TPU v7x, 32 devices: a whole 2x2x4 slice. The times are simulated.
32 devices in a mesh: groups: 2 (over x), ctx: 8 (over z, y), head: 2 (over core).
Axes of the slice: x: 2, y: 2, z: 4, core: 2. Of those that a mesh axis runs over, the one named last changes fastest.
Arguments:
- queries: bfloat16 [4096, 20, 128], P(('groups', 'ctx'), 'head'), parts along dimension 0, may hold values from -70 to 70, as said below
- keys: bfloat16 [4096, 4, 128], P(('groups', 'ctx'), 'head'), parts along dimension 0, may hold values from -3.5 to 3.5
- doc_lengths: int32 [8], P('groups'), parts along dimension 0, may hold values from 1 to 24, 32 in all
- gate_query_weight: bfloat16 [20, 128, 128], P('head'), may hold values from -0.5 to 0.5
- gate_key_weight: bfloat16 [4, 384, 128], P('head'), may hold values from -0.3125 to 0.3125
Outputs:
- block_targets: float32 [20, 64, 32], P('head', ('groups', 'ctx')), parts along dimension 1
- key_proj_grad: float32 [64, 4, 128], P(('groups', 'ctx'), 'head'), parts along dimension 0
- query_weight_grad: float32 [40, 128, 128], P(('groups', 'head')), parts along dimension 0
- key_weight_grad: float32 [8, 384, 128], P(('groups', 'head')), parts along dimension 0
There are 2 independent parts, one for each index of `groups`. A program takes and returns all parts, laid end to end along the dimension named above; an argument that names none is the same for every part. Nothing has to cross between parts.
Inputs may be any that keep to these rules, and one draw needn't show every extreme that they name: queries are of order one except in a few rows.
All inputs are finite; a program needn't handle non-finite values.
Results may differ from a plain program's by a relative error of at most 0.006.
Values may be sent and summed in bfloat16 or wider, within the bound.
No kernel may reach another device: no remote copies, remote signals or barrier semaphores. Data moves between devices by JAX's collectives and lax.ppermute only.
A program may use at most 64 MiB of HBM per device.

v0:
```python
import functools
import math

import jax
import jax.numpy as jnp
from jax import lax
from jax.experimental import pallas as pl
from jax.experimental.pallas import tpu as pltpu
from jax.sharding import PartitionSpec as P

BLK = 64
LANES = 128
LOG2E = 1.4426950408889634
LOW = -1e30
VMEM_LIMIT = 24 * 1024 * 1024
F32 = jnp.float32
BF16 = jnp.bfloat16


def dot(a, b, a_dim, b_dim, precision=None):
    return lax.dot_general(
        a, b, (((a_dim,), (b_dim,)), ((), ())), precision=precision, preferred_element_type=F32
    )


def halves(value):
    high = value.astype(BF16)
    return high, (value - high.astype(F32)).astype(BF16)


def iota(shape, dim):
    return lax.broadcasted_iota(jnp.int32, shape, dim)


def doc_begins(lengths_ref):
    begins, total = [], jnp.int32(0)
    for doc in range(lengths_ref.shape[0]):
        begins.append(total)
        total = total + lengths_ref[doc]
    return begins


def start_of(begins, block):
    start = jnp.zeros_like(block)
    for begin in begins:
        start = jnp.maximum(start, jnp.where(begin <= block, begin, 0))
    return start


def pool_keys(piece_ref, out_ref, at, head_size):
    rows, width = piece_ref.shape
    keys = piece_ref[...].astype(F32).reshape(rows // BLK, BLK, width)
    stats = (jnp.max(keys, 1), jnp.min(keys, 1), jnp.sum(keys, 1) * (1.0 / BLK))
    for group in range(width // head_size):
        for part, value in enumerate(stats):
            out_ref[group, at, :, part * head_size : (part + 1) * head_size] = value[
                :, group * head_size : (group + 1) * head_size
            ]


def absorb(scale, begins, me, step, piece_ref, q_ref, best_ref, sum_ref, at):
    heads, rows, head_size = q_ref.shape
    kv = piece_ref.shape[1] // head_size
    blocks = rows // BLK
    source = me ^ step
    needed = (source <= me) & (source * blocks + blocks > start_of(begins, me * blocks))

    @pl.when(needed)
    def _():
        if step == 0:
            causal = iota((rows, rows), 0) <= iota((rows, rows), 1)
        for head in range(heads):
            group = head // (heads // kv)
            key_rows = piece_ref[:, group * head_size : (group + 1) * head_size]
            scores = dot(key_rows, q_ref[head], 1, 1)
            if step == 0:
                scores = jnp.where(causal, scores, LOW)
            scores = scores.reshape(blocks, BLK, rows)
            best = jnp.max(scores, axis=1)
            best_ref[head, at : at + blocks, :] = best
            sum_ref[head, at : at + blocks, :] = jnp.sum(
                jnp.exp2((scores - best[:, None, :]) * scale), axis=1
            )


def absorb_together(scale, begins, me, steps, pieces, q_ref, best_ref, sum_ref):
    heads, rows, head_size = q_ref.shape
    kv = pieces[0].shape[1] // head_size
    blocks = rows // BLK
    first_needed = start_of(begins, me * blocks)
    needed = False
    for step in steps:
        source = me ^ step
        needed |= (source <= me) & (source * blocks + blocks > first_needed)

    @pl.when(needed)
    def _():
        for group in range(kv):
            lanes = slice(group * head_size, (group + 1) * head_size)
            key_rows = jnp.concatenate([piece_ref[:, lanes] for piece_ref in pieces], axis=0)
            for head in range(group * heads // kv, (group + 1) * heads // kv):
                scores = dot(key_rows, q_ref[head], 1, 1).reshape(-1, BLK, rows)
                best = jnp.max(scores, axis=1)
                best_ref[head] = best
                sum_ref[head] = jnp.sum(
                    jnp.exp2((scores - best[:, None, :]) * scale), axis=1
                )


def own_kernel(
    scale, lengths_ref, far_q_ref, far_wq_ref, own_ref,
    q_ref, wq_ref, best_ref, sum_ref, pk_ref, pq_ref, proj_ref, kept_lengths_ref, copied,
):
    heads, rows, head_size = q_ref.shape
    blocks = rows // BLK
    me = lax.axis_index("ctx")
    begins = doc_begins(lengths_ref)
    q_copy = pltpu.make_async_copy(far_q_ref, q_ref, copied.at[0])
    wq_copy = pltpu.make_async_copy(far_wq_ref, wq_ref, copied.at[1])
    q_copy.start()
    wq_copy.start()
    for doc in range(lengths_ref.shape[0]):
        kept_lengths_ref[doc] = lengths_ref[doc]
    pool_keys(own_ref, pk_ref, 0, head_size)
    q_copy.wait()
    wq_copy.wait()
    for head in range(heads):
        values = q_ref[head].astype(F32).reshape(blocks, BLK, head_size)
        pooled = (jnp.sum(values, axis=1) * (1.0 / BLK)).astype(BF16)
        pq_ref[head * blocks : (head + 1) * blocks, :] = pooled.astype(F32)
        proj_ref[head * blocks : (head + 1) * blocks, :] = dot(pooled, wq_ref[head], 1, 0)
    absorb(scale, begins, me, 0, own_ref, q_ref, best_ref, sum_ref, 0)


def direct_kernel(scale, steps, lengths_ref, q_ref, *refs):
    pieces = refs[: len(steps)]
    best_ref, sum_ref, pk_ref = refs[len(steps) :]
    _, rows, head_size = q_ref.shape
    blocks = rows // BLK
    me = lax.axis_index("ctx")
    begins = doc_begins(lengths_ref)
    for at, (step, piece_ref) in enumerate(zip(steps, pieces)):
        pool_keys(piece_ref, pk_ref, at, head_size)
        absorb(scale, begins, me, step, piece_ref, q_ref, best_ref, sum_ref, at * blocks)


def late_kernel(scale, gate_scale, direct_steps, late_steps, lengths_ref, q_ref, wk_ref, *refs):
    count = len(late_steps)
    pieces = refs[:count]
    own_best_ref, own_sum_ref, own_pk_ref, pq_ref, proj_ref = refs[count : count + 5]
    best_ref, sum_ref, pk_ref = refs[count + 5 : count + 8]
    targets_ref, sent_ref, pooled_k_ref, key_proj_ref = refs[count + 8 : count + 12]
    late_best_ref, late_sum_ref, late_pk_ref, all_pk_ref, column_ref = refs[count + 12 :]
    heads, rows, head_size = q_ref.shape
    kv = wk_ref.shape[0]
    blocks = rows // BLK
    steps = (0,) + tuple(direct_steps) + tuple(late_steps)
    ranks = len(steps)
    block_count = blocks * ranks
    own_rows = heads * blocks
    me = lax.axis_index("ctx")
    begins = doc_begins(lengths_ref)
    absorb_together(
        scale, begins, me, late_steps, pieces, q_ref, late_best_ref, late_sum_ref
    )

    for at, piece_ref in enumerate(pieces):
        pool_keys(piece_ref, late_pk_ref, at, head_size)
    for group in range(kv):
        for at, step in enumerate(steps):
            if at < 1:
                value = own_pk_ref[group, at]
            elif at < 1 + len(direct_steps):
                value = pk_ref[group, at - 1]
            else:
                value = late_pk_ref[group, at - 1 - len(direct_steps)]
            all_pk_ref[group, me ^ step] = value
    proj_high, proj_low = halves(proj_ref[...])
    proj = jnp.concatenate([proj_high, proj_high, proj_low], axis=1)
    logits = jnp.zeros((own_rows, block_count), F32)
    row = iota((own_rows, block_count), 0)
    for group in range(kv):
        pooled_k = all_pk_ref[group].reshape(block_count, 3 * head_size).astype(BF16)
        key_proj = dot(pooled_k, wk_ref[group], 1, 0)
        pooled_k_ref[group] = pooled_k
        key_proj_ref[group] = key_proj
        key_high, key_low = halves(key_proj)
        part = dot(proj, jnp.concatenate([key_high, key_low, key_high], axis=1), 1, 1)
        logits = jnp.where(row // (own_rows // kv) == group, part, logits)
    query_block = me * blocks + row % blocks
    key_block = iota((own_rows, block_count), 1)
    allowed = (key_block <= query_block) & (key_block >= start_of(begins, query_block))
    logits = jnp.where(allowed, logits * gate_scale, LOW)
    weights = jnp.exp(logits - jnp.max(logits, axis=1, keepdims=True))
    probs = weights / jnp.sum(weights, axis=1, keepdims=True)

    stat_row = iota((block_count, rows), 0)
    key_block = (me ^ (stat_row // blocks)) * blocks + stat_row % blocks
    lane_block = me * blocks + iota((block_count, rows), 1) // BLK
    valid = (key_block <= lane_block) & (key_block >= start_of(begins, lane_block))
    lane = iota((block_count, LANES), 1)
    half_lane = lane // BLK
    columns = jnp.zeros((block_count, LANES), F32)
    for head in range(heads):
        best = [own_best_ref[head], best_ref[head], late_best_ref[head]]
        total = [own_sum_ref[head], sum_ref[head], late_sum_ref[head]]
        best, total = jnp.concatenate(best, axis=0), jnp.concatenate(total, axis=0)
        best = jnp.where(valid, best, LOW)
        shifted = (best - jnp.max(best, axis=0, keepdims=True)) * scale
        total = jnp.sum(jnp.where(valid, total, 0.0) * jnp.exp2(shifted), axis=0, keepdims=True)
        ratio = shifted - jnp.log2(total)
        for block in range(blocks):
            tile = block * BLK // LANES
            inside = half_lane == block % (LANES // BLK)
            part = jnp.where(inside, ratio[:, tile * LANES : (tile + 1) * LANES], LOW)
            high = jnp.max(part, axis=1, keepdims=True)
            columns = jnp.where(lane == head * blocks + block, high, columns)
    raw = jnp.exp2(columns)
    raw = raw * (1.0 / jnp.sum(raw, axis=0, keepdims=True))
    for at, step in enumerate(steps):
        column_ref[me ^ step] = raw[at * blocks : (at + 1) * blocks]
    final = column_ref[...].reshape(block_count, LANES)
    if block_count < LANES:
        final = jnp.concatenate([final, jnp.zeros((LANES - block_count, LANES), F32)], axis=0)
    targets = final.T[0:own_rows, 0:block_count]
    for head in range(heads):
        targets_ref[head] = targets[head * blocks : (head + 1) * blocks]

    delta = jnp.where(allowed, probs - targets, 0.0)
    high, low = halves(delta)
    pieces_of_row = [high.astype(F32), low.astype(F32)]
    width = sent_ref.shape[1]
    if width > 2 * block_count:
        pieces_of_row.append(jnp.zeros((own_rows, width - 2 * block_count), F32))
    pooled_q = pq_ref[...]
    if width > head_size:
        pooled_q = jnp.concatenate(
            [pooled_q, jnp.zeros((own_rows, width - head_size), F32)], axis=1
        )
    packed = jnp.concatenate([pooled_q, jnp.concatenate(pieces_of_row, axis=1)], axis=0)
    sent_ref[...] = packed.astype(BF16)


def join_kernel(own_ref, side_ref, joined_ref):
    joined_ref[0] = own_ref[...]
    joined_ref[1] = side_ref[...]


def gate_kernel(scale, count, *refs):
    packed = jnp.concatenate([ref[...].astype(F32) for ref in refs[:count]], axis=0)
    own_targets_ref, pooled_k_ref, key_proj_ref, wq_ref = refs[count : count + 4]
    targets_ref, key_grad_ref, wq_grad_ref, wk_grad_ref, own_ref = refs[count + 4 :]
    targets_ref[...] = own_targets_ref[...]
    ranks, packed_rows, _ = packed.shape
    kv, block_count, _ = pooled_k_ref.shape
    heads, head_size, _ = wq_ref.shape
    repeats = heads // kv
    blocks = block_count // ranks
    me = lax.axis_index("ctx")
    for group in range(kv):
        key_high, key_low = halves(key_proj_ref[group] * scale)
        both_keys = jnp.concatenate([key_high, key_high], axis=0)
        pooled, deltas, projected = [], [], []
        for head in range(group * repeats, (group + 1) * repeats):
            rows = packed[:, head * blocks : (head + 1) * blocks, 0:head_size]
            pooled.append(rows.reshape(block_count, head_size).astype(BF16))
            at = packed_rows // 2 + head * blocks
            rows = packed[:, at : at + blocks, :].reshape(block_count, -1)
            deltas.append(rows[:, 0 : 2 * block_count].astype(BF16))
            projected.append(dot(pooled[-1], wq_ref[head], 1, 0))
        delta = jnp.concatenate(deltas, axis=0)
        delta_high = delta[:, 0:block_count]
        query_grad = dot(delta, both_keys, 1, 0) + dot(delta_high, key_low, 1, 0)
        grad_high, grad_low = halves(query_grad)
        for at in range(repeats):
            rows = slice(at * block_count, (at + 1) * block_count)
            wq_grad_ref[group * repeats + at] = dot(
                jnp.concatenate([pooled[at], pooled[at]], axis=0),
                jnp.concatenate([grad_high[rows], grad_low[rows]], axis=0),
                0,
                0,
            )
        proj_high, proj_low = halves(jnp.concatenate(projected, axis=0) * scale)
        main = dot(delta, proj_high, 0, 0)
        key_grad = main[0:block_count] + main[block_count:] + dot(delta_high, proj_low, 0, 0)
        grad_high, grad_low = halves(key_grad)
        pooled_k = pooled_k_ref[group]
        wk_grad_ref[group] = dot(
            jnp.concatenate([pooled_k, pooled_k], axis=0),
            jnp.concatenate([grad_high, grad_low], axis=0),
            0,
            0,
        )
        own_ref[...] = key_grad.reshape(ranks, blocks, head_size)
        key_grad_ref[:, group, :] = own_ref[me]


def per_device(queries, keys, doc_lengths, gate_query_weight, gate_key_weight):
    rows, heads, head_size = queries.shape
    kv = keys.shape[1]
    ranks = lax.axis_size("ctx")
    blocks = rows // BLK
    block_count = blocks * ranks
    own_rows = heads * blocks
    scale = LOG2E / math.sqrt(head_size)
    gate_scale = 1.0 / math.sqrt(gate_query_weight.shape[2])
    params = pltpu.CompilerParams(vmem_limit_bytes=VMEM_LIMIT)
    smem = pl.BlockSpec(memory_space=pltpu.SMEM)
    vmem = pl.BlockSpec(memory_space=pltpu.VMEM)
    anywhere = pl.BlockSpec(memory_space=pltpu.HBM)

    def near(value):
        return pltpu.with_memory_space_constraint(value, pltpu.VMEM)

    def distant(value):
        return pltpu.with_memory_space_constraint(value, pltpu.HBM)

    def exchange(value, step):
        return lax.ppermute(value, "ctx", [(i, i ^ step) for i in range(ranks)])

    flat_keys = keys.reshape(rows, kv * head_size)
    head_queries = queries.transpose(1, 0, 2)
    pool_width = 3 * head_size
    own_stats = pltpu.VMEM((heads, blocks, rows), F32)
    *near_values, own_best, own_sum, own_pk, pooled_q, proj, lengths = pl.pallas_call(
        functools.partial(own_kernel, scale),
        out_shape=(
            pltpu.VMEM(head_queries.shape, BF16),
            pltpu.VMEM(gate_query_weight.shape, BF16),
            own_stats,
            own_stats,
            pltpu.VMEM((kv, 1, blocks, pool_width), F32),
            pltpu.VMEM((own_rows, head_size), F32),
            pltpu.VMEM((own_rows, head_size), F32),
            pltpu.SMEM(doc_lengths.shape, jnp.int32),
        ),
        in_specs=[smem, anywhere, anywhere, vmem],
        out_specs=(vmem,) * 7 + (smem,),
        scratch_shapes=[pltpu.SemaphoreType.DMA((2,))],
        compiler_params=params,
        name="own_key_blocks",
    )(doc_lengths, distant(head_queries), distant(gate_query_weight), near(flat_keys))
    near_q, near_wq = (near(value) for value in near_values)
    lengths = pltpu.with_memory_space_constraint(lengths, pltpu.SMEM)

    far = ranks // 2
    direct_steps = list(range(1, far + 1))
    late_steps = list(range(far + 1, ranks))
    pieces = {0: flat_keys}
    for step in direct_steps:
        pieces[step] = exchange(flat_keys, step)
    for step in late_steps:
        pieces[step] = exchange(pieces[far], step - far)
    pieces = {step: near(piece) for step, piece in pieces.items()}
    stats = pltpu.VMEM((heads, len(direct_steps) * blocks, rows), F32)
    late_stats = pltpu.VMEM((heads, len(late_steps) * blocks, rows), F32)
    direct = pl.pallas_call(
        functools.partial(direct_kernel, scale, direct_steps),
        out_shape=(
            stats,
            stats,
            pltpu.VMEM((kv, len(direct_steps), blocks, pool_width), F32),
        ),
        in_specs=[smem] + [vmem] * (1 + len(direct_steps)),
        out_specs=(vmem,) * 3,
        compiler_params=params,
        name="direct_key_blocks",
    )(lengths, near_q, *[pieces[s] for s in direct_steps])
    width = -(-2 * block_count // LANES) * LANES
    block_targets, sent, pooled_k, key_proj = pl.pallas_call(
        functools.partial(late_kernel, scale, gate_scale, direct_steps, late_steps),
        out_shape=(
            pltpu.VMEM((heads, blocks, block_count), F32),
            pltpu.VMEM((2 * own_rows, width), BF16),
            pltpu.VMEM((kv, block_count, pool_width), BF16),
            pltpu.VMEM((kv, block_count, head_size), F32),
        ),
        in_specs=[smem] + [vmem] * (10 + len(late_steps)),
        out_specs=(vmem,) * 4,
        scratch_shapes=[
            late_stats,
            late_stats,
            pltpu.VMEM((kv, len(late_steps), blocks, pool_width), F32),
            pltpu.VMEM((kv, ranks, blocks, pool_width), F32),
            pltpu.VMEM((ranks, blocks, LANES), F32),
        ],
        compiler_params=params,
        name="late_key_blocks",
    )(
        lengths,
        near_q,
        near(gate_key_weight),
        *[pieces[s] for s in late_steps],
        *[near(value) for value in (own_best, own_sum, own_pk, pooled_q, proj, *direct)],
    )
    joined = pl.pallas_call(
        join_kernel,
        out_shape=pltpu.VMEM((2, *sent.shape), BF16),
        in_specs=[vmem, vmem],
        out_specs=vmem,
        compiler_params=params,
        name="join_neighbours",
    )(near(sent), near(exchange(sent, 1)))
    packed = [joined] + [exchange(joined, step) for step in range(2, ranks, 2)]
    return pl.pallas_call(
        functools.partial(gate_kernel, gate_scale, len(packed)),
        out_shape=(
            jax.ShapeDtypeStruct((heads, blocks, block_count), F32),
            jax.ShapeDtypeStruct((blocks, kv, head_size), F32),
            jax.ShapeDtypeStruct(gate_query_weight.shape, F32),
            jax.ShapeDtypeStruct(gate_key_weight.shape, F32),
        ),
        in_specs=[vmem] * (4 + len(packed)),
        out_specs=(vmem,) * 4,
        scratch_shapes=[pltpu.VMEM((ranks, blocks, head_size), F32)],
        compiler_params=params,
        name="gate_gradients",
    )(
        *[near(value) for value in packed],
        near(block_targets),
        near(pooled_k),
        near(key_proj),
        near_wq,
    )


def solution(mesh):
    placed = (
        P(("groups", "ctx"), "head", None),
        P(("groups", "ctx"), "head", None),
        P("groups"),
        P("head", None, None),
        P("head", None, None),
    )
    return jax.shard_map(
        per_device,
        mesh=mesh,
        in_specs=placed,
        out_specs=(
            P("head", ("groups", "ctx"), None),
            P(("groups", "ctx"), "head", None),
            P(("groups", "head"), None, None),
            P(("groups", "head"), None, None),
        ),
        check_vma=False,
    )
```

profile of v0, /device:TPU:0, one launch (start us, length us, event | category | flops | bytes accessed | tf_op | source)
XLA Modules:
  0.0 38.5 jit_solution(5843092239245816950)
XLA Ops:
  0.6 0.9 %copy.11 = bf16[32,8,2,128]{3,1,2,0:T(8,128)(2,1)S(1)} copy(bf16[32,8,2,128]{3,2,1,0:T(2,128)(2,1)} %bitcast.11) | data formatting | bytes 262144
  1.6 0.0 copy-start.1
  1.6 4.1 %collective-permute-start = (bf16[256,256]{1,0:T(8,128)(2,1)S(1)}, bf16[256,256]{1,0:T(8,128)(2,1)S(1)}, u32[]{:S(2)}, u32[]{:S(2)}) collective-permute-start(bf16[256,256]{1,0:T(8,128)(2,1)S(1)} %bitcast.5), channel_id=1, source_target_pairs={{0,8},{2,10},{4,12},{6,14},{8,0},{10,2},{12,4},{14,6},{1,9},{3,11}... | collective-permute-start | bytes 393224 | tf_op jit(solution)/shard_map/ppermute | solution.py:319
  5.7 1.5 %collective-permute-start.4 = (bf16[256,256]{1,0:T(8,128)(2,1)S(1)}, bf16[256,256]{1,0:T(8,128)(2,1)S(1)}, u32[]{:S(2)}, u32[]{:S(2)}) collective-permute-start(bf16[256,256]{1,0:T(8,128)(2,1)S(1)} %bitcast.6), channel_id=1, source_target_pairs={{0,2},{2,0},{4,6},{6,4},{8,10},{10,8},{12,14},{14,12},{1,3},{3,1},... | collective-permute-start | bytes 393224 | tf_op jit(solution)/shard_map/ppermute | solution.py:319
  7.2 1.6 %collective-permute-start.5 = (bf16[256,256]{1,0:T(8,128)(2,1)S(1)}, bf16[256,256]{1,0:T(8,128)(2,1)S(1)}, u32[]{:S(2)}, u32[]{:S(2)}) collective-permute-start(bf16[256,256]{1,0:T(8,128)(2,1)S(1)} %bitcast.7), channel_id=1, source_target_pairs={{0,4},{2,6},{4,0},{6,2},{8,12},{10,14},{12,8},{14,10},{1,5},{3,7},... | collective-permute-start | bytes 393224 | tf_op jit(solution)/shard_map/ppermute | solution.py:319
  8.8 0.4 %collective-permute-start.6 = (bf16[256,256]{1,0:T(8,128)(2,1)S(1)}, bf16[256,256]{1,0:T(8,128)(2,1)S(1)}, u32[]{:S(2)}, u32[]{:S(2)}) collective-permute-start(bf16[256,256]{1,0:T(8,128)(2,1)S(1)} %bitcast.8), channel_id=1, source_target_pairs={{0,6},{2,4},{4,2},{6,0},{8,14},{10,12},{12,10},{14,8},{1,7},{3,5},... | collective-permute-start | bytes 393224 | tf_op jit(solution)/shard_map/ppermute | solution.py:319
  9.2 2.9 %collective-permute-done.refs_3_ = bf16[256,256]{1,0:T(8,128)(2,1)S(1)} collective-permute-done((bf16[256,256]{1,0:T(8,128)(2,1)S(1)}, bf16[256,256]{1,0:T(8,128)(2,1)S(1)}, u32[]{:S(2)}, u32[]{:S(2)}) %collective-permute-start) | collective-permute-done | bytes 131104 | tf_op jit(solution)/shard_map/ppermute | solution.py:319
  12.1 1.6 %collective-permute-start.1 = (bf16[256,256]{1,0:T(8,128)(2,1)S(1)}, bf16[256,256]{1,0:T(8,128)(2,1)S(1)}, u32[]{:S(2)}, u32[]{:S(2)}) collective-permute-start(bf16[256,256]{1,0:T(8,128)(2,1)S(1)} %collective-permute-done.refs_3_), channel_id=1, source_target_pairs={{0,2},{2,0},{4,6},{6,4},{8,10},{10,8},{12,14},{14,12},{1,3},{3,1},... | collective-permute-start | bytes 393224 | tf_op jit(solution)/shard_map/ppermute | solution.py:319
  13.6 0.6 %collective-permute-start.2 = (bf16[256,256]{1,0:T(8,128)(2,1)S(1)}, bf16[256,256]{1,0:T(8,128)(2,1)S(1)}, u32[]{:S(2)}, u32[]{:S(2)}) collective-permute-start(bf16[256,256]{1,0:T(8,128)(2,1)S(1)} %collective-permute-done.refs_3_), channel_id=1, source_target_pairs={{0,4},{2,6},{4,0},{6,2},{8,12},{10,14},{12,8},{14,10},{1,5},{3,7},... | collective-permute-start | bytes 393224 | tf_op jit(solution)/shard_map/ppermute | solution.py:319
  14.3 0.0 collective-permute-done.4.refs_0_
  14.3 1.3 %collective-permute-start.3 = (bf16[256,256]{1,0:T(8,128)(2,1)S(1)}, bf16[256,256]{1,0:T(8,128)(2,1)S(1)}, u32[]{:S(2)}, u32[]{:S(2)}) collective-permute-start(bf16[256,256]{1,0:T(8,128)(2,1)S(1)} %collective-permute-done.refs_3_), channel_id=1, source_target_pairs={{0,6},{2,4},{4,2},{6,0},{8,14},{10,12},{12,10},{14,8},{1,7},{3,5},... | collective-permute-start | bytes 393224 | tf_op jit(solution)/shard_map/ppermute | solution.py:319
  15.6 0.0 copy-done.1
  15.6 2.7 %own_key_blocks.1 = (bf16[10,256,128]{2,1,0:T(8,128)(2,1)S(1)}, bf16[10,128,128]{2,1,0:T(8,128)(2,1)S(1)}, f32[10,4,256]{2,1,0:T(4,128)S(1)}, f32[10,4,256]{2,1,...) custom-call(s32[4]{0:T(128)S(1)} %copy-done.1, ...), custom_call_target="tpu_custom_call" | custom-call | tf_op jit(solution)/shard_map/own_key_blocks/pallas_call | solution.py:325
  18.3 0.0 collective-permute-done.5.refs_1_
  18.3 0.0 collective-permute-done.6.refs_2_
  18.3 0.0 copy-start
  18.3 0.2 direct_key_blocks.1
  18.6 0.6 %collective-permute-done.1.refs_0_ = bf16[256,256]{1,0:T(8,128)(2,1)S(1)} collective-permute-done((bf16[256,256]{1,0:T(8,128)(2,1)S(1)}, bf16[256,256]{1,0:T(8,128)(2,1)S(1)}, u32[]{:S(2)}, u32[]{:S(2)}) %collective-permute-start.1) | collective-permute-done | bytes 131104 | tf_op jit(solution)/shard_map/ppermute | solution.py:319
  19.2 0.9 %collective-permute-done.2.refs_1_ = bf16[256,256]{1,0:T(8,128)(2,1)S(1)} collective-permute-done((bf16[256,256]{1,0:T(8,128)(2,1)S(1)}, bf16[256,256]{1,0:T(8,128)(2,1)S(1)}, u32[]{:S(2)}, u32[]{:S(2)}) %collective-permute-start.2) | collective-permute-done | bytes 131104 | tf_op jit(solution)/shard_map/ppermute | solution.py:319
  20.2 1.8 %collective-permute-done.3.refs_2_ = bf16[256,256]{1,0:T(8,128)(2,1)S(1)} collective-permute-done((bf16[256,256]{1,0:T(8,128)(2,1)S(1)}, bf16[256,256]{1,0:T(8,128)(2,1)S(1)}, u32[]{:S(2)}, u32[]{:S(2)}) %collective-permute-start.3) | collective-permute-done | bytes 131104 | tf_op jit(solution)/shard_map/ppermute | solution.py:319
  22.0 0.0 copy-done
  22.0 1.0 %late_key_blocks.1 = (f32[10,4,32]{2,1,0:T(4,128)S(1)}, bf16[80,128]{1,0:T(8,128)(2,1)S(1)}, bf16[2,32,384]{2,1,0:T(8,128)(2,1)S(1)}, f32[2,32,128]{2,1,0:T(8,128)S(1)}) custom-call(s32[4]{0:T(128)S(4)} %get-tuple-element.19.lengths_ref, bf16[10,256,128]{2,1,0:T(8,128)(2,1)S(1)} %get-tuple-element.20.q_ref, bf16[2,384,128]{2,1,0:T(8,128)(2,1)S(1)} %copy-done, ...), custom_call_target="tpu_custom_call" | custom-call | tf_op jit(solution)/shard_map/late_key_blocks/pallas_call | solution.py:370
  23.0 1.4 %collective-permute-start.7 = (bf16[80,128]{1,0:T(8,128)(2,1)S(1)}, bf16[80,128]{1,0:T(8,128)(2,1)S(1)}, u32[]{:S(2)}, u32[]{:S(2)}) collective-permute-start(bf16[80,128]{1,0:T(8,128)(2,1)S(1)} %get-tuple-element.29.own_ref), channel_id=1, source_target_pairs={{0,2},{2,0},{4,6},{6,4},{8,10},{10,8},{12,14},{14,12},{1,3},{3,1},... | collective-permute-start | bytes 61448 | tf_op jit(solution)/shard_map/ppermute | solution.py:319
  24.4 2.4 %collective-permute-done.7.side_ref = bf16[80,128]{1,0:T(8,128)(2,1)S(1)} collective-permute-done((bf16[80,128]{1,0:T(8,128)(2,1)S(1)}, bf16[80,128]{1,0:T(8,128)(2,1)S(1)}, u32[]{:S(2)}, u32[]{:S(2)}) %collective-permute-start.7) | collective-permute-done | bytes 20512 | tf_op jit(solution)/shard_map/ppermute | solution.py:319
  26.8 5.0 %collective-permute-start.10 = (bf16[2,80,128]{2,1,0:T(8,128)(2,1)S(1)}, bf16[2,80,128]{2,1,0:T(8,128)(2,1)S(1)}, u32[]{:S(2)}, u32[]{:S(2)}) collective-permute-start(bf16[2,80,128]{2,1,0:T(8,128)(2,1)S(1)} %join_neighbours.1.refs_0_), channel_id=1, source_target_pairs={{0,12},{2,14},{4,8},{6,10},{8,4},{10,6},{12,0},{14,2},{1,13},{3,15... | collective-permute-start | bytes 122888 | tf_op jit(solution)/shard_map/ppermute | solution.py:319
  31.8 0.0 collective-permute-start.8
  31.8 0.6 %collective-permute-start.9 = (bf16[2,80,128]{2,1,0:T(8,128)(2,1)S(1)}, bf16[2,80,128]{2,1,0:T(8,128)(2,1)S(1)}, u32[]{:S(2)}, u32[]{:S(2)}) collective-permute-start(bf16[2,80,128]{2,1,0:T(8,128)(2,1)S(1)} %join_neighbours.1.refs_0_), channel_id=1, source_target_pairs={{0,8},{2,10},{4,12},{6,14},{8,0},{10,2},{12,4},{14,6},{1,9},{3,11}... | collective-permute-start | bytes 122888 | tf_op jit(solution)/shard_map/ppermute | solution.py:319
  32.4 1.5 %collective-permute-done.10.refs_3_ = bf16[2,80,128]{2,1,0:T(8,128)(2,1)S(1)} collective-permute-done((bf16[2,80,128]{2,1,0:T(8,128)(2,1)S(1)}, bf16[2,80,128]{2,1,0:T(8,128)(2,1)S(1)}, u32[]{:S(2)}, u32[]{:S(2)}) %collective-permute-start.10) | collective-permute-done | bytes 40992 | tf_op jit(solution)/shard_map/ppermute | solution.py:319
  33.8 1.9 %collective-permute-done.8.refs_1_ = bf16[2,80,128]{2,1,0:T(8,128)(2,1)S(1)} collective-permute-done((bf16[2,80,128]{2,1,0:T(8,128)(2,1)S(1)}, bf16[2,80,128]{2,1,0:T(8,128)(2,1)S(1)}, u32[]{:S(2)}, u32[]{:S(2)}) %collective-permute-start.8) | collective-permute-done | bytes 40992 | tf_op jit(solution)/shard_map/ppermute | solution.py:319
  35.8 0.9 %collective-permute-done.9.refs_2_ = bf16[2,80,128]{2,1,0:T(8,128)(2,1)S(1)} collective-permute-done((bf16[2,80,128]{2,1,0:T(8,128)(2,1)S(1)}, bf16[2,80,128]{2,1,0:T(8,128)(2,1)S(1)}, u32[]{:S(2)}, u32[]{:S(2)}) %collective-permute-start.9) | collective-permute-done | bytes 40992 | tf_op jit(solution)/shard_map/ppermute | solution.py:319
  36.7 1.8 %gate_gradients.1 = (f32[10,4,32]{2,1,0:T(4,128)}, f32[4,2,128]{2,1,0:T(2,128)}, f32[10,128,128]{2,1,0:T(8,128)}, f32[2,384,128]{2,1,0:T(8,128)}) custom-call(bf16[2,80,128]{2,1,0:T(8,128)(2,1)S(1)} %join_neighbours.1.refs_0_, bf16[2,80,128]{2,1,0:T(8,128)(2,1)S(1)} %collective-permute-done.8.refs_1_, ...), custom_call_target="tpu_custom_call" | custom-call | tf_op jit(solution)/shard_map/gate_gradients/pallas_call | solution.py:405
  (1 shorter events, 0.0 us)
Async XLA Ops:
  1.6 14.0 %copy-start.1 = (s32[4]{0:T(128)S(1)}, s32[4]{0:T(128)}, u32[]{:S(2)}) copy-start(s32[4]{0:T(128)} %lengths_ref.1) | copy-start | bytes 52
  1.6 10.5 %collective-permute-start = (bf16[256,256]{1,0:T(8,128)(2,1)S(1)}, bf16[256,256]{1,0:T(8,128)(2,1)S(1)}, u32[]{:S(2)}, u32[]{:S(2)}) collective-permute-start(bf16[256,256]{1,0:T(8,128)(2,1)S(1)} %bitcast.5), channel_id=1, source_target_pairs={{0,8},{2,10},{4,12},{6,14},{8,0},{10,2},{12,4},{14,6},{1,9},{3,11}... | collective-permute-start | bytes 393224 | tf_op jit(solution)/shard_map/ppermute | solution.py:319
  5.7 8.6 %collective-permute-start.4 = (bf16[256,256]{1,0:T(8,128)(2,1)S(1)}, bf16[256,256]{1,0:T(8,128)(2,1)S(1)}, u32[]{:S(2)}, u32[]{:S(2)}) collective-permute-start(bf16[256,256]{1,0:T(8,128)(2,1)S(1)} %bitcast.6), channel_id=1, source_target_pairs={{0,2},{2,0},{4,6},{6,4},{8,10},{10,8},{12,14},{14,12},{1,3},{3,1},... | collective-permute-start | bytes 393224 | tf_op jit(solution)/shard_map/ppermute | solution.py:319
  7.2 11.1 %collective-permute-start.5 = (bf16[256,256]{1,0:T(8,128)(2,1)S(1)}, bf16[256,256]{1,0:T(8,128)(2,1)S(1)}, u32[]{:S(2)}, u32[]{:S(2)}) collective-permute-start(bf16[256,256]{1,0:T(8,128)(2,1)S(1)} %bitcast.7), channel_id=1, source_target_pairs={{0,4},{2,6},{4,0},{6,2},{8,12},{10,14},{12,8},{14,10},{1,5},{3,7},... | collective-permute-start | bytes 393224 | tf_op jit(solution)/shard_map/ppermute | solution.py:319
  8.8 9.6 %collective-permute-start.6 = (bf16[256,256]{1,0:T(8,128)(2,1)S(1)}, bf16[256,256]{1,0:T(8,128)(2,1)S(1)}, u32[]{:S(2)}, u32[]{:S(2)}) collective-permute-start(bf16[256,256]{1,0:T(8,128)(2,1)S(1)} %bitcast.8), channel_id=1, source_target_pairs={{0,6},{2,4},{4,2},{6,0},{8,14},{10,12},{12,10},{14,8},{1,7},{3,5},... | collective-permute-start | bytes 393224 | tf_op jit(solution)/shard_map/ppermute | solution.py:319
  12.1 7.1 %collective-permute-start.1 = (bf16[256,256]{1,0:T(8,128)(2,1)S(1)}, bf16[256,256]{1,0:T(8,128)(2,1)S(1)}, u32[]{:S(2)}, u32[]{:S(2)}) collective-permute-start(bf16[256,256]{1,0:T(8,128)(2,1)S(1)} %collective-permute-done.refs_3_), channel_id=1, source_target_pairs={{0,2},{2,0},{4,6},{6,4},{8,10},{10,8},{12,14},{14,12},{1,3},{3,1},... | collective-permute-start | bytes 393224 | tf_op jit(solution)/shard_map/ppermute | solution.py:319
  13.6 6.5 %collective-permute-start.2 = (bf16[256,256]{1,0:T(8,128)(2,1)S(1)}, bf16[256,256]{1,0:T(8,128)(2,1)S(1)}, u32[]{:S(2)}, u32[]{:S(2)}) collective-permute-start(bf16[256,256]{1,0:T(8,128)(2,1)S(1)} %collective-permute-done.refs_3_), channel_id=1, source_target_pairs={{0,4},{2,6},{4,0},{6,2},{8,12},{10,14},{12,8},{14,10},{1,5},{3,7},... | collective-permute-start | bytes 393224 | tf_op jit(solution)/shard_map/ppermute | solution.py:319
  14.3 7.7 %collective-permute-start.3 = (bf16[256,256]{1,0:T(8,128)(2,1)S(1)}, bf16[256,256]{1,0:T(8,128)(2,1)S(1)}, u32[]{:S(2)}, u32[]{:S(2)}) collective-permute-start(bf16[256,256]{1,0:T(8,128)(2,1)S(1)} %collective-permute-done.refs_3_), channel_id=1, source_target_pairs={{0,6},{2,4},{4,2},{6,0},{8,14},{10,12},{12,10},{14,8},{1,7},{3,5},... | collective-permute-start | bytes 393224 | tf_op jit(solution)/shard_map/ppermute | solution.py:319
  18.3 3.7 %copy-start = (bf16[2,384,128]{2,1,0:T(8,128)(2,1)S(1)}, bf16[2,384,128]{2,1,0:T(8,128)(2,1)}, u32[]{:S(2)}) copy-start(bf16[2,384,128]{2,1,0:T(8,128)(2,1)} %wk_ref.1) | copy-start | bytes 589828
  23.0 3.8 %collective-permute-start.7 = (bf16[80,128]{1,0:T(8,128)(2,1)S(1)}, bf16[80,128]{1,0:T(8,128)(2,1)S(1)}, u32[]{:S(2)}, u32[]{:S(2)}) collective-permute-start(bf16[80,128]{1,0:T(8,128)(2,1)S(1)} %get-tuple-element.29.own_ref), channel_id=1, source_target_pairs={{0,2},{2,0},{4,6},{6,4},{8,10},{10,8},{12,14},{14,12},{1,3},{3,1},... | collective-permute-start | bytes 61448 | tf_op jit(solution)/shard_map/ppermute | solution.py:319
  26.8 7.0 %collective-permute-start.10 = (bf16[2,80,128]{2,1,0:T(8,128)(2,1)S(1)}, bf16[2,80,128]{2,1,0:T(8,128)(2,1)S(1)}, u32[]{:S(2)}, u32[]{:S(2)}) collective-permute-start(bf16[2,80,128]{2,1,0:T(8,128)(2,1)S(1)} %join_neighbours.1.refs_0_), channel_id=1, source_target_pairs={{0,12},{2,14},{4,8},{6,10},{8,4},{10,6},{12,0},{14,2},{1,13},{3,15... | collective-permute-start | bytes 122888 | tf_op jit(solution)/shard_map/ppermute | solution.py:319
  31.8 4.0 %collective-permute-start.8 = (bf16[2,80,128]{2,1,0:T(8,128)(2,1)S(1)}, bf16[2,80,128]{2,1,0:T(8,128)(2,1)S(1)}, u32[]{:S(2)}, u32[]{:S(2)}) collective-permute-start(bf16[2,80,128]{2,1,0:T(8,128)(2,1)S(1)} %join_neighbours.1.refs_0_), channel_id=1, source_target_pairs={{0,4},{2,6},{4,0},{6,2},{8,12},{10,14},{12,8},{14,10},{1,5},{3,7},... | collective-permute-start | bytes 122888 | tf_op jit(solution)/shard_map/ppermute | solution.py:319
  31.8 4.9 %collective-permute-start.9 = (bf16[2,80,128]{2,1,0:T(8,128)(2,1)S(1)}, bf16[2,80,128]{2,1,0:T(8,128)(2,1)S(1)}, u32[]{:S(2)}, u32[]{:S(2)}) collective-permute-start(bf16[2,80,128]{2,1,0:T(8,128)(2,1)S(1)} %join_neighbours.1.refs_0_), channel_id=1, source_target_pairs={{0,8},{2,10},{4,12},{6,14},{8,0},{10,2},{12,4},{14,6},{1,9},{3,11}... | collective-permute-start | bytes 122888 | tf_op jit(solution)/shard_map/ppermute | solution.py:319
where the time goes:
time: 38.6 us; the launch traced here: 38.5 us
  starting transfers between devices  18.1 us (47%)
  waiting for transfers between devices  13 us (34%)
  Pallas kernels  5.75 us (15%)
  local copies, waits for them, and re-layouts  0.94 us (2%)
  between operations  0.69 us (2%)
    ppermute x11, starting transfers between devices, exchange(): return lax.ppermute(value, 'ctx', [(i, i ^ step) for i in range(ranks)])  18.1 us
    ppermute x11, waiting for transfers between devices, exchange(): return lax.ppermute(value, 'ctx', [(i, i ^ step) for i in range(ranks)])  13 us
    pallas_call x1, Pallas kernels, per_device(): pl.pallas_call(functools.partial(own_kernel, scale), out_shape=(pltpu.VME...  2.72 us
    pallas_call x1, Pallas kernels, per_device(): pl.pallas_call(functools.partial(gate_kernel, gate_scale, len(packed)), o...  1.79 us
    pallas_call x1, Pallas kernels, per_device(): pl.pallas_call(functools.partial(late_kernel, scale, gate_scale, direct_s...  0.98 us
    unnamed x5, local copies, waits for them, and re-layouts  0.94 us
  transfers between devices with their start and end apart: 11, of which 8 were waited for; matrix products, arithmetic and copies ran while one was open for 0% of the time, Pallas kernels for 8%

commit v1 on v0

--- a/solution.py
+++ b/solution.py
@@ -130,6 +130,10 @@
         pq_ref[head * blocks : (head + 1) * blocks, :] = pooled.astype(F32)
         proj_ref[head * blocks : (head + 1) * blocks, :] = dot(pooled, wq_ref[head], 1, 0)
     absorb(scale, begins, me, 0, own_ref, q_ref, best_ref, sum_ref, 0)
+
+
+def pass_kernel(marker_ref, *refs):
+    del marker_ref, refs
 
 
 def direct_kernel(scale, steps, lengths_ref, q_ref, *refs):
@@ -343,13 +347,27 @@
     near_q, near_wq = (near(value) for value in near_values)
     lengths = pltpu.with_memory_space_constraint(lengths, pltpu.SMEM)
 
+    def after(marker, *values):
+        return pl.pallas_call(
+            pass_kernel,
+            out_shape=tuple(pltpu.VMEM(value.shape, BF16) for value in values),
+            in_specs=[smem] + [vmem] * len(values),
+            out_specs=(vmem,) * len(values),
+            input_output_aliases={1 + at: at for at in range(len(values))},
+            compiler_params=params,
+            name="pass_on",
+        )(marker, *[near(value) for value in values])
+
     far = ranks // 2
+    pieces = {0: flat_keys}
+    for step in [far, *range(2, far, 2), 1]:
+        pieces[step] = exchange(flat_keys, step)
+    (pieces[far],) = after(lengths, pieces[far])
+    for step in range(3, far, 2):
+        pieces[step] = exchange(pieces[step - 1], 1)
     direct_steps = list(range(1, far + 1))
-    late_steps = list(range(far + 1, ranks))
-    pieces = {0: flat_keys}
-    for step in direct_steps:
-        pieces[step] = exchange(flat_keys, step)
-    for step in late_steps:
+    late_steps = [step for step in range(1, ranks) if step not in direct_steps]
+    for step in range(far + 1, ranks):
         pieces[step] = exchange(pieces[far], step - far)
     pieces = {step: near(piece) for step, piece in pieces.items()}
     stats = pltpu.VMEM((heads, len(direct_steps) * blocks, rows), F32)

time: 38.6 us -> 36 us (0.933)
  starting transfers between devices: 18.1 us -> 16.8 us
  waiting for transfers between devices: 13 us -> 11.7 us
    ppermute x11, starting transfers between devices: 18.1 us -> 16.8 us  [exchange(): return lax.ppermute(value, 'ctx', [(i, i ^ step) for i in range(ranks)])]
    ppermute x11, waiting for transfers between devices: 13 us -> 11.7 us  [exchange(): return lax.ppermute(value, 'ctx', [(i, i ^ step) for i in range(ranks)])]
where the time goes in v1:
time: 36 us; the launch traced here: 35.9 us
  starting transfers between devices  16.8 us (47%)
  waiting for transfers between devices  11.7 us (32%)
  Pallas kernels  5.75 us (16%)
  local copies, waits for them, and re-layouts  0.93 us (3%)
  between operations  0.68 us (2%)
    ppermute x11, starting transfers between devices, exchange(): return lax.ppermute(value, 'ctx', [(i, i ^ step) for i in range(ranks)])  16.8 us
    ppermute x11, waiting for transfers between devices, exchange(): return lax.ppermute(value, 'ctx', [(i, i ^ step) for i in range(ranks)])  11.7 us
    pallas_call x1, Pallas kernels, per_device(): pl.pallas_call(functools.partial(own_kernel, scale), out_shape=(pltpu.VME...  2.72 us
    pallas_call x1, Pallas kernels, per_device(): pl.pallas_call(functools.partial(gate_kernel, gate_scale, len(packed)), o...  1.79 us
    pallas_call x1, Pallas kernels, per_device(): pl.pallas_call(functools.partial(late_kernel, scale, gate_scale, direct_s...  0.98 us
    unnamed x5, local copies, waits for them, and re-layouts  0.93 us
  transfers between devices with their start and end apart: 11, of which 8 were waited for; matrix products, arithmetic and copies ran while one was open for 0% of the time, Pallas kernels for 8%

profile of v1, /device:TPU:0, one launch (start us, length us, event | category | flops | bytes accessed | tf_op | source)
XLA Modules:
  0.0 35.9 jit_solution(6889423801006181154)
XLA Ops:
  0.6 0.9 %copy.12 = bf16[32,8,2,128]{3,1,2,0:T(8,128)(2,1)S(1)} copy(bf16[32,8,2,128]{3,2,1,0:T(2,128)(2,1)} %bitcast.10) | data formatting | bytes 262144
  1.6 0.0 copy-start.1
  1.6 3.1 %collective-permute-start.5 = (bf16[256,256]{1,0:T(8,128)(2,1)S(1)}, bf16[256,256]{1,0:T(8,128)(2,1)S(1)}, u32[]{:S(2)}, u32[]{:S(2)}) collective-permute-start(bf16[256,256]{1,0:T(8,128)(2,1)S(1)} %bitcast.5), channel_id=1, source_target_pairs={{0,4},{2,6},{4,0},{6,2},{8,12},{10,14},{12,8},{14,10},{1,5},{3,7},... | collective-permute-start | bytes 393224 | tf_op jit(solution)/shard_map/ppermute | solution.py:323
  4.7 2.6 %collective-permute-start = (bf16[256,256]{1,0:T(8,128)(2,1)S(1)}, bf16[256,256]{1,0:T(8,128)(2,1)S(1)}, u32[]{:S(2)}, u32[]{:S(2)}) collective-permute-start(bf16[256,256]{1,0:T(8,128)(2,1)S(1)} %bitcast.6), channel_id=1, source_target_pairs={{0,8},{2,10},{4,12},{6,14},{8,0},{10,2},{12,4},{14,6},{1,9},{3,11}... | collective-permute-start | bytes 393224 | tf_op jit(solution)/shard_map/ppermute | solution.py:323
  7.2 1.5 %collective-permute-start.4 = (bf16[256,256]{1,0:T(8,128)(2,1)S(1)}, bf16[256,256]{1,0:T(8,128)(2,1)S(1)}, u32[]{:S(2)}, u32[]{:S(2)}) collective-permute-start(bf16[256,256]{1,0:T(8,128)(2,1)S(1)} %bitcast.7), channel_id=1, source_target_pairs={{0,2},{2,0},{4,6},{6,4},{8,10},{10,8},{12,14},{14,12},{1,3},{3,1},... | collective-permute-start | bytes 393224 | tf_op jit(solution)/shard_map/ppermute | solution.py:323
  8.8 0.0 copy-done.1
  8.8 2.7 %own_key_blocks.1 = (bf16[10,256,128]{2,1,0:T(8,128)(2,1)S(1)}, bf16[10,128,128]{2,1,0:T(8,128)(2,1)S(1)}, f32[10,4,256]{2,1,0:T(4,128)S(1)}, f32[10,4,256]{2,1,...) custom-call(s32[4]{0:T(128)S(1)} %copy-done.1, ...), custom_call_target="tpu_custom_call" | custom-call | tf_op jit(solution)/shard_map/own_key_blocks/pallas_call | solution.py:329
  11.5 0.0 collective-permute-done.5.refs_1_
  11.5 0.6 %collective-permute-start.6 = (bf16[256,256]{1,0:T(8,128)(2,1)S(1)}, bf16[256,256]{1,0:T(8,128)(2,1)S(1)}, u32[]{:S(2)}, u32[]{:S(2)}) collective-permute-start(bf16[256,256]{1,0:T(8,128)(2,1)S(1)} %collective-permute-done.5.refs_1_), channel_id=1, source_target_pairs={{0,2},{2,0},{4,6},{6,4},{8,10},{10,8},{12,14},{14,12},{1,3},{3,1},... | collective-permute-start | bytes 393224 | tf_op jit(solution)/shard_map/ppermute | solution.py:323
  12.1 1.3 %collective-permute-done.refs_0_ = bf16[256,256]{1,0:T(8,128)(2,1)S(1)} collective-permute-done((bf16[256,256]{1,0:T(8,128)(2,1)S(1)}, bf16[256,256]{1,0:T(8,128)(2,1)S(1)}, u32[]{:S(2)}, u32[]{:S(2)}) %collective-permute-start) | collective-permute-done | bytes 131104 | tf_op jit(solution)/shard_map/ppermute | solution.py:323
  13.4 1.4 %collective-permute-start.3 = (bf16[256,256]{1,0:T(8,128)(2,1)S(1)}, bf16[256,256]{1,0:T(8,128)(2,1)S(1)}, u32[]{:S(2)}, u32[]{:S(2)}) collective-permute-start(bf16[256,256]{1,0:T(8,128)(2,1)S(1)} %pass_on.1.refs_3_), channel_id=1, source_target_pairs={{0,6},{2,4},{4,2},{6,0},{8,14},{10,12},{12,10},{14,8},{1,7},{3,5},... | collective-permute-start | bytes 393224 | tf_op jit(solution)/shard_map/ppermute | solution.py:323
  14.8 1.6 %collective-permute-start.2 = (bf16[256,256]{1,0:T(8,128)(2,1)S(1)}, bf16[256,256]{1,0:T(8,128)(2,1)S(1)}, u32[]{:S(2)}, u32[]{:S(2)}) collective-permute-start(bf16[256,256]{1,0:T(8,128)(2,1)S(1)} %pass_on.1.refs_3_), channel_id=1, source_target_pairs={{0,4},{2,6},{4,0},{6,2},{8,12},{10,14},{12,8},{14,10},{1,5},{3,7},... | collective-permute-start | bytes 393224 | tf_op jit(solution)/shard_map/ppermute | solution.py:323
  16.4 0.5 %collective-permute-start.1 = (bf16[256,256]{1,0:T(8,128)(2,1)S(1)}, bf16[256,256]{1,0:T(8,128)(2,1)S(1)}, u32[]{:S(2)}, u32[]{:S(2)}) collective-permute-start(bf16[256,256]{1,0:T(8,128)(2,1)S(1)} %pass_on.1.refs_3_), channel_id=1, source_target_pairs={{0,2},{2,0},{4,6},{6,4},{8,10},{10,8},{12,14},{14,12},{1,3},{3,1},... | collective-permute-start | bytes 393224 | tf_op jit(solution)/shard_map/ppermute | solution.py:323
  16.9 0.0 collective-permute-done.4.refs_0_
  16.9 3.3 %collective-permute-done.6.refs_2_ = bf16[256,256]{1,0:T(8,128)(2,1)S(1)} collective-permute-done((bf16[256,256]{1,0:T(8,128)(2,1)S(1)}, bf16[256,256]{1,0:T(8,128)(2,1)S(1)}, u32[]{:S(2)}, u32[]{:S(2)}) %collective-permute-start.6) | collective-permute-done | bytes 131104 | tf_op jit(solution)/shard_map/ppermute | solution.py:323
  20.2 0.0 copy-start
  20.2 0.2 direct_key_blocks.1
  20.4 0.0 collective-permute-done.3.refs_2_
  20.4 0.3 collective-permute-done.2.refs_1_
  20.7 0.8 %collective-permute-done.1.refs_0_ = bf16[256,256]{1,0:T(8,128)(2,1)S(1)} collective-permute-done((bf16[256,256]{1,0:T(8,128)(2,1)S(1)}, bf16[256,256]{1,0:T(8,128)(2,1)S(1)}, u32[]{:S(2)}, u32[]{:S(2)}) %collective-permute-start.1) | collective-permute-done | bytes 131104 | tf_op jit(solution)/shard_map/ppermute | solution.py:323
  21.6 0.0 copy-done
  21.6 1.0 %late_key_blocks.1 = (f32[10,4,32]{2,1,0:T(4,128)S(1)}, bf16[80,128]{1,0:T(8,128)(2,1)S(1)}, bf16[2,32,384]{2,1,0:T(8,128)(2,1)S(1)}, f32[2,32,128]{2,1,0:T(8,128)S(1)}) custom-call(s32[4]{0:T(128)S(4)} %get-tuple-element.19.marker_ref.lengths_ref, bf16[10,256,128]{2,1,0:T(8,128)(2,1)S(1)} %get-tuple-element.20.q_ref, bf16[2,384,128]{2,1,0:T(8,128)(2,1)S(1)} %copy-done, ...), custom_call_target="tpu_custom_call" | custom-call | tf_op jit(solution)/shard_map/late_key_blocks/pallas_call | solution.py:388
  22.6 1.1 %collective-permute-start.7 = (bf16[80,128]{1,0:T(8,128)(2,1)S(1)}, bf16[80,128]{1,0:T(8,128)(2,1)S(1)}, u32[]{:S(2)}, u32[]{:S(2)}) collective-permute-start(bf16[80,128]{1,0:T(8,128)(2,1)S(1)} %get-tuple-element.29.own_ref), channel_id=1, source_target_pairs={{0,2},{2,0},{4,6},{6,4},{8,10},{10,8},{12,14},{14,12},{1,3},{3,1},... | collective-permute-start | bytes 61448 | tf_op jit(solution)/shard_map/ppermute | solution.py:323
  23.7 2.7 %collective-permute-done.7.side_ref = bf16[80,128]{1,0:T(8,128)(2,1)S(1)} collective-permute-done((bf16[80,128]{1,0:T(8,128)(2,1)S(1)}, bf16[80,128]{1,0:T(8,128)(2,1)S(1)}, u32[]{:S(2)}, u32[]{:S(2)}) %collective-permute-start.7) | collective-permute-done | bytes 20512 | tf_op jit(solution)/shard_map/ppermute | solution.py:323
  26.4 2.5 %collective-permute-start.10 = (bf16[2,80,128]{2,1,0:T(8,128)(2,1)S(1)}, bf16[2,80,128]{2,1,0:T(8,128)(2,1)S(1)}, u32[]{:S(2)}, u32[]{:S(2)}) collective-permute-start(bf16[2,80,128]{2,1,0:T(8,128)(2,1)S(1)} %join_neighbours.1.refs_0_), channel_id=1, source_target_pairs={{0,12},{2,14},{4,8},{6,10},{8,4},{10,6},{12,0},{14,2},{1,13},{3,15... | collective-permute-start | bytes 122888 | tf_op jit(solution)/shard_map/ppermute | solution.py:323
  28.9 0.7 %collective-permute-start.9 = (bf16[2,80,128]{2,1,0:T(8,128)(2,1)S(1)}, bf16[2,80,128]{2,1,0:T(8,128)(2,1)S(1)}, u32[]{:S(2)}, u32[]{:S(2)}) collective-permute-start(bf16[2,80,128]{2,1,0:T(8,128)(2,1)S(1)} %join_neighbours.1.refs_0_), channel_id=1, source_target_pairs={{0,8},{2,10},{4,12},{6,14},{8,0},{10,2},{12,4},{14,6},{1,9},{3,11}... | collective-permute-start | bytes 122888 | tf_op jit(solution)/shard_map/ppermute | solution.py:323
  29.6 1.2 %collective-permute-start.8 = (bf16[2,80,128]{2,1,0:T(8,128)(2,1)S(1)}, bf16[2,80,128]{2,1,0:T(8,128)(2,1)S(1)}, u32[]{:S(2)}, u32[]{:S(2)}) collective-permute-start(bf16[2,80,128]{2,1,0:T(8,128)(2,1)S(1)} %join_neighbours.1.refs_0_), channel_id=1, source_target_pairs={{0,4},{2,6},{4,0},{6,2},{8,12},{10,14},{12,8},{14,10},{1,5},{3,7},... | collective-permute-start | bytes 122888 | tf_op jit(solution)/shard_map/ppermute | solution.py:323
  30.8 1.4 %collective-permute-done.10.refs_3_ = bf16[2,80,128]{2,1,0:T(8,128)(2,1)S(1)} collective-permute-done((bf16[2,80,128]{2,1,0:T(8,128)(2,1)S(1)}, bf16[2,80,128]{2,1,0:T(8,128)(2,1)S(1)}, u32[]{:S(2)}, u32[]{:S(2)}) %collective-permute-start.10) | collective-permute-done | bytes 40992 | tf_op jit(solution)/shard_map/ppermute | solution.py:323
  32.2 1.7 %collective-permute-done.9.refs_2_ = bf16[2,80,128]{2,1,0:T(8,128)(2,1)S(1)} collective-permute-done((bf16[2,80,128]{2,1,0:T(8,128)(2,1)S(1)}, bf16[2,80,128]{2,1,0:T(8,128)(2,1)S(1)}, u32[]{:S(2)}, u32[]{:S(2)}) %collective-permute-start.9) | collective-permute-done | bytes 40992 | tf_op jit(solution)/shard_map/ppermute | solution.py:323
  33.9 0.2 collective-permute-done.8.refs_1_
  34.1 1.8 %gate_gradients.1 = (f32[10,4,32]{2,1,0:T(4,128)}, f32[4,2,128]{2,1,0:T(2,128)}, f32[10,128,128]{2,1,0:T(8,128)}, f32[2,384,128]{2,1,0:T(8,128)}) custom-call(bf16[2,80,128]{2,1,0:T(8,128)(2,1)S(1)} %join_neighbours.1.refs_0_, bf16[2,80,128]{2,1,0:T(8,128)(2,1)S(1)} %collective-permute-done.8.refs_1_, ...), custom_call_target="tpu_custom_call" | custom-call | tf_op jit(solution)/shard_map/gate_gradients/pallas_call | solution.py:423
  (2 shorter events, 0.0 us)
Async XLA Ops:
  1.6 7.2 %copy-start.1 = (s32[4]{0:T(128)S(1)}, s32[4]{0:T(128)}, u32[]{:S(2)}) copy-start(s32[4]{0:T(128)} %lengths_ref.1) | copy-start | bytes 52
  1.6 9.9 %collective-permute-start.5 = (bf16[256,256]{1,0:T(8,128)(2,1)S(1)}, bf16[256,256]{1,0:T(8,128)(2,1)S(1)}, u32[]{:S(2)}, u32[]{:S(2)}) collective-permute-start(bf16[256,256]{1,0:T(8,128)(2,1)S(1)} %bitcast.5), channel_id=1, source_target_pairs={{0,4},{2,6},{4,0},{6,2},{8,12},{10,14},{12,8},{14,10},{1,5},{3,7},... | collective-permute-start | bytes 393224 | tf_op jit(solution)/shard_map/ppermute | solution.py:323
  4.7 8.7 %collective-permute-start = (bf16[256,256]{1,0:T(8,128)(2,1)S(1)}, bf16[256,256]{1,0:T(8,128)(2,1)S(1)}, u32[]{:S(2)}, u32[]{:S(2)}) collective-permute-start(bf16[256,256]{1,0:T(8,128)(2,1)S(1)} %bitcast.6), channel_id=1, source_target_pairs={{0,8},{2,10},{4,12},{6,14},{8,0},{10,2},{12,4},{14,6},{1,9},{3,11}... | collective-permute-start | bytes 393224 | tf_op jit(solution)/shard_map/ppermute | solution.py:323
  7.2 9.6 %collective-permute-start.4 = (bf16[256,256]{1,0:T(8,128)(2,1)S(1)}, bf16[256,256]{1,0:T(8,128)(2,1)S(1)}, u32[]{:S(2)}, u32[]{:S(2)}) collective-permute-start(bf16[256,256]{1,0:T(8,128)(2,1)S(1)} %bitcast.7), channel_id=1, source_target_pairs={{0,2},{2,0},{4,6},{6,4},{8,10},{10,8},{12,14},{14,12},{1,3},{3,1},... | collective-permute-start | bytes 393224 | tf_op jit(solution)/shard_map/ppermute | solution.py:323
  11.5 8.7 %collective-permute-start.6 = (bf16[256,256]{1,0:T(8,128)(2,1)S(1)}, bf16[256,256]{1,0:T(8,128)(2,1)S(1)}, u32[]{:S(2)}, u32[]{:S(2)}) collective-permute-start(bf16[256,256]{1,0:T(8,128)(2,1)S(1)} %collective-permute-done.5.refs_1_), channel_id=1, source_target_pairs={{0,2},{2,0},{4,6},{6,4},{8,10},{10,8},{12,14},{14,12},{1,3},{3,1},... | collective-permute-start | bytes 393224 | tf_op jit(solution)/shard_map/ppermute | solution.py:323
  13.4 7.0 %collective-permute-start.3 = (bf16[256,256]{1,0:T(8,128)(2,1)S(1)}, bf16[256,256]{1,0:T(8,128)(2,1)S(1)}, u32[]{:S(2)}, u32[]{:S(2)}) collective-permute-start(bf16[256,256]{1,0:T(8,128)(2,1)S(1)} %pass_on.1.refs_3_), channel_id=1, source_target_pairs={{0,6},{2,4},{4,2},{6,0},{8,14},{10,12},{12,10},{14,8},{1,7},{3,5},... | collective-permute-start | bytes 393224 | tf_op jit(solution)/shard_map/ppermute | solution.py:323
  14.8 6.0 %collective-permute-start.2 = (bf16[256,256]{1,0:T(8,128)(2,1)S(1)}, bf16[256,256]{1,0:T(8,128)(2,1)S(1)}, u32[]{:S(2)}, u32[]{:S(2)}) collective-permute-start(bf16[256,256]{1,0:T(8,128)(2,1)S(1)} %pass_on.1.refs_3_), channel_id=1, source_target_pairs={{0,4},{2,6},{4,0},{6,2},{8,12},{10,14},{12,8},{14,10},{1,5},{3,7},... | collective-permute-start | bytes 393224 | tf_op jit(solution)/shard_map/ppermute | solution.py:323
  16.4 5.2 %collective-permute-start.1 = (bf16[256,256]{1,0:T(8,128)(2,1)S(1)}, bf16[256,256]{1,0:T(8,128)(2,1)S(1)}, u32[]{:S(2)}, u32[]{:S(2)}) collective-permute-start(bf16[256,256]{1,0:T(8,128)(2,1)S(1)} %pass_on.1.refs_3_), channel_id=1, source_target_pairs={{0,2},{2,0},{4,6},{6,4},{8,10},{10,8},{12,14},{14,12},{1,3},{3,1},... | collective-permute-start | bytes 393224 | tf_op jit(solution)/shard_map/ppermute | solution.py:323
  20.2 1.4 %copy-start = (bf16[2,384,128]{2,1,0:T(8,128)(2,1)S(1)}, bf16[2,384,128]{2,1,0:T(8,128)(2,1)}, u32[]{:S(2)}) copy-start(bf16[2,384,128]{2,1,0:T(8,128)(2,1)} %wk_ref.1) | copy-start | bytes 589828
  22.6 3.8 %collective-permute-start.7 = (bf16[80,128]{1,0:T(8,128)(2,1)S(1)}, bf16[80,128]{1,0:T(8,128)(2,1)S(1)}, u32[]{:S(2)}, u32[]{:S(2)}) collective-permute-start(bf16[80,128]{1,0:T(8,128)(2,1)S(1)} %get-tuple-element.29.own_ref), channel_id=1, source_target_pairs={{0,2},{2,0},{4,6},{6,4},{8,10},{10,8},{12,14},{14,12},{1,3},{3,1},... | collective-permute-start | bytes 61448 | tf_op jit(solution)/shard_map/ppermute | solution.py:323
  26.4 5.8 %collective-permute-start.10 = (bf16[2,80,128]{2,1,0:T(8,128)(2,1)S(1)}, bf16[2,80,128]{2,1,0:T(8,128)(2,1)S(1)}, u32[]{:S(2)}, u32[]{:S(2)}) collective-permute-start(bf16[2,80,128]{2,1,0:T(8,128)(2,1)S(1)} %join_neighbours.1.refs_0_), channel_id=1, source_target_pairs={{0,12},{2,14},{4,8},{6,10},{8,4},{10,6},{12,0},{14,2},{1,13},{3,15... | collective-permute-start | bytes 122888 | tf_op jit(solution)/shard_map/ppermute | solution.py:323
  28.9 5.0 %collective-permute-start.9 = (bf16[2,80,128]{2,1,0:T(8,128)(2,1)S(1)}, bf16[2,80,128]{2,1,0:T(8,128)(2,1)S(1)}, u32[]{:S(2)}, u32[]{:S(2)}) collective-permute-start(bf16[2,80,128]{2,1,0:T(8,128)(2,1)S(1)} %join_neighbours.1.refs_0_), channel_id=1, source_target_pairs={{0,8},{2,10},{4,12},{6,14},{8,0},{10,2},{12,4},{14,6},{1,9},{3,11}... | collective-permute-start | bytes 122888 | tf_op jit(solution)/shard_map/ppermute | solution.py:323
  29.6 4.4 %collective-permute-start.8 = (bf16[2,80,128]{2,1,0:T(8,128)(2,1)S(1)}, bf16[2,80,128]{2,1,0:T(8,128)(2,1)S(1)}, u32[]{:S(2)}, u32[]{:S(2)}) collective-permute-start(bf16[2,80,128]{2,1,0:T(8,128)(2,1)S(1)} %join_neighbours.1.refs_0_), channel_id=1, source_target_pairs={{0,4},{2,6},{4,0},{6,2},{8,12},{10,14},{12,8},{14,10},{1,5},{3,7},... | collective-permute-start | bytes 122888 | tf_op jit(solution)/shard_map/ppermute | solution.py:323

commit v2 on v1

--- a/solution.py
+++ b/solution.py
@@ -136,29 +136,33 @@
     del marker_ref, refs
 
 
-def direct_kernel(scale, steps, lengths_ref, q_ref, *refs):
+def pieces_kernel(scale, steps, lengths_ref, q_ref, earlier_ref, *refs):
+    del earlier_ref
     pieces = refs[: len(steps)]
     best_ref, sum_ref, pk_ref = refs[len(steps) :]
     _, rows, head_size = q_ref.shape
     blocks = rows // BLK
     me = lax.axis_index("ctx")
     begins = doc_begins(lengths_ref)
-    for at, (step, piece_ref) in enumerate(zip(steps, pieces)):
+    for at, piece_ref in enumerate(pieces):
         pool_keys(piece_ref, pk_ref, at, head_size)
-        absorb(scale, begins, me, step, piece_ref, q_ref, best_ref, sum_ref, at * blocks)
-
-
-def late_kernel(scale, gate_scale, direct_steps, late_steps, lengths_ref, q_ref, wk_ref, *refs):
+    absorb_together(scale, begins, me, steps, pieces, q_ref, best_ref, sum_ref)
+
+
+def late_kernel(
+    scale, gate_scale, first_steps, middle_steps, late_steps, lengths_ref, q_ref, wk_ref, *refs
+):
     count = len(late_steps)
     pieces = refs[:count]
     own_best_ref, own_sum_ref, own_pk_ref, pq_ref, proj_ref = refs[count : count + 5]
-    best_ref, sum_ref, pk_ref = refs[count + 5 : count + 8]
-    targets_ref, sent_ref, pooled_k_ref, key_proj_ref = refs[count + 8 : count + 12]
-    late_best_ref, late_sum_ref, late_pk_ref, all_pk_ref, column_ref = refs[count + 12 :]
+    first_best_ref, first_sum_ref, first_pk_ref = refs[count + 5 : count + 8]
+    middle_best_ref, middle_sum_ref, middle_pk_ref = refs[count + 8 : count + 11]
+    targets_ref, sent_ref, pooled_k_ref, key_proj_ref = refs[count + 11 : count + 15]
+    late_best_ref, late_sum_ref, late_pk_ref, all_pk_ref, column_ref = refs[count + 15 :]
     heads, rows, head_size = q_ref.shape
     kv = wk_ref.shape[0]
     blocks = rows // BLK
-    steps = (0,) + tuple(direct_steps) + tuple(late_steps)
+    steps = (0, *middle_steps, *late_steps, *first_steps)
     ranks = len(steps)
     block_count = blocks * ranks
     own_rows = heads * blocks
@@ -171,13 +175,10 @@
     for at, piece_ref in enumerate(pieces):
         pool_keys(piece_ref, late_pk_ref, at, head_size)
     for group in range(kv):
-        for at, step in enumerate(steps):
-            if at < 1:
-                value = own_pk_ref[group, at]
-            elif at < 1 + len(direct_steps):
-                value = pk_ref[group, at - 1]
-            else:
-                value = late_pk_ref[group, at - 1 - len(direct_steps)]
+        pooled = [own_pk_ref[group, 0]]
+        for ref in (middle_pk_ref, late_pk_ref, first_pk_ref):
+            pooled += [ref[group, at] for at in range(ref.shape[1])]
+        for step, value in zip(steps, pooled):
             all_pk_ref[group, me ^ step] = value
     proj_high, proj_low = halves(proj_ref[...])
     proj = jnp.concatenate([proj_high, proj_high, proj_low], axis=1)
@@ -199,16 +200,20 @@
     probs = weights / jnp.sum(weights, axis=1, keepdims=True)
 
     stat_row = iota((block_count, rows), 0)
-    key_block = (me ^ (stat_row // blocks)) * blocks + stat_row % blocks
+    step_of_row = jnp.zeros_like(stat_row)
+    for at, step in enumerate(steps):
+        step_of_row = jnp.where(stat_row // blocks == at, step, step_of_row)
+    key_block = (me ^ step_of_row) * blocks + stat_row % blocks
     lane_block = me * blocks + iota((block_count, rows), 1) // BLK
     valid = (key_block <= lane_block) & (key_block >= start_of(begins, lane_block))
     lane = iota((block_count, LANES), 1)
     half_lane = lane // BLK
     columns = jnp.zeros((block_count, LANES), F32)
     for head in range(heads):
-        best = [own_best_ref[head], best_ref[head], late_best_ref[head]]
-        total = [own_sum_ref[head], sum_ref[head], late_sum_ref[head]]
-        best, total = jnp.concatenate(best, axis=0), jnp.concatenate(total, axis=0)
+        best = (own_best_ref, middle_best_ref, late_best_ref, first_best_ref)
+        total = (own_sum_ref, middle_sum_ref, late_sum_ref, first_sum_ref)
+        best = jnp.concatenate([ref[head] for ref in best], axis=0)
+        total = jnp.concatenate([ref[head] for ref in total], axis=0)
         best = jnp.where(valid, best, LOW)
         shifted = (best - jnp.max(best, axis=0, keepdims=True)) * scale
         total = jnp.sum(jnp.where(valid, total, 0.0) * jnp.exp2(shifted), axis=0, keepdims=True)
@@ -366,34 +371,41 @@
     for step in range(3, far, 2):
         pieces[step] = exchange(pieces[step - 1], 1)
     direct_steps = list(range(1, far + 1))
-    late_steps = [step for step in range(1, ranks) if step not in direct_steps]
+    middle_steps = [ranks - 1]
+    late_steps = list(range(far + 1, ranks - 1))
     for step in range(far + 1, ranks):
         pieces[step] = exchange(pieces[far], step - far)
     pieces = {step: near(piece) for step, piece in pieces.items()}
-    stats = pltpu.VMEM((heads, len(direct_steps) * blocks, rows), F32)
+
+    def absorb_pieces(steps, earlier, name):
+        stats = pltpu.VMEM((heads, len(steps) * blocks, rows), F32)
+        values = pl.pallas_call(
+            functools.partial(pieces_kernel, scale, steps),
+            out_shape=(
+                stats,
+                stats,
+                pltpu.VMEM((kv, len(steps), blocks, pool_width), F32),
+            ),
+            in_specs=[smem] + [vmem] * (2 + len(steps)),
+            out_specs=(vmem,) * 3,
+            compiler_params=params,
+            name=name,
+        )(lengths, near_q, earlier, *[pieces[s] for s in steps])
+        return [near(value) for value in values]
+
+    direct = absorb_pieces(direct_steps, near(own_sum), "direct_key_blocks")
+    middle = absorb_pieces(middle_steps, direct[0], "middle_key_blocks")
     late_stats = pltpu.VMEM((heads, len(late_steps) * blocks, rows), F32)
-    direct = pl.pallas_call(
-        functools.partial(direct_kernel, scale, direct_steps),
-        out_shape=(
-            stats,
-            stats,
-            pltpu.VMEM((kv, len(direct_steps), blocks, pool_width), F32),
-        ),
-        in_specs=[smem] + [vmem] * (1 + len(direct_steps)),
-        out_specs=(vmem,) * 3,
-        compiler_params=params,
-        name="direct_key_blocks",
-    )(lengths, near_q, *[pieces[s] for s in direct_steps])
     width = -(-2 * block_count // LANES) * LANES
     block_targets, sent, pooled_k, key_proj = pl.pallas_call(
-        functools.partial(late_kernel, scale, gate_scale, direct_steps, late_steps),
+        functools.partial(late_kernel, scale, gate_scale, direct_steps, middle_steps, late_steps),
         out_shape=(
             pltpu.VMEM((heads, blocks, block_count), F32),
             pltpu.VMEM((2 * own_rows, width), BF16),
             pltpu.VMEM((kv, block_count, pool_width), BF16),
             pltpu.VMEM((kv, block_count, head_size), F32),
         ),
-        in_specs=[smem] + [vmem] * (10 + len(late_steps)),
+        in_specs=[smem] + [vmem] * (13 + len(late_steps)),
         out_specs=(vmem,) * 4,
         scratch_shapes=[
             late_stats,
@@ -409,7 +421,9 @@
         near_q,
         near(gate_key_weight),
         *[pieces[s] for s in late_steps],
-        *[near(value) for value in (own_best, own_sum, own_pk, pooled_q, proj, *direct)],
+        *[near(value) for value in (own_best, own_sum, own_pk, pooled_q, proj)],
+        *direct,
+        *middle,
     )
     joined = pl.pallas_call(
         join_kernel,

time: 36 us -> 36.7 us (1.019); the launches traced: 35.9 us -> 37 us
  starting transfers between devices: 16.8 us -> 18.9 us
  waiting for transfers between devices: 11.7 us -> 10.7 us
    ppermute x11, starting transfers between devices: 16.8 us -> 18.9 us  [exchange(): return lax.ppermute(value, 'ctx', [(i, i ^ step) for i in range(ranks)])]
    ppermute x11, waiting for transfers between devices: 11.7 us -> 10.7 us  [exchange(): return lax.ppermute(value, 'ctx', [(i, i ^ step) for i in range(ranks)])]
  transfers between devices with their start and end apart: 11 -> 11, of which waited for: 8 -> 7; matrix products, arithmetic and copies ran while one was open for 0% -> 0% of each run, Pallas kernels for 8% -> 8%
where the time goes in v2:
time: 36.7 us; the launch traced here: 37 us
  starting transfers between devices  18.9 us (51%)
  waiting for transfers between devices  10.7 us (29%)
  Pallas kernels  5.73 us (16%)
  local copies, waits for them, and re-layouts  0.94 us (3%)
  between operations  0.7 us (2%)
    ppermute x11, starting transfers between devices, exchange(): return lax.ppermute(value, 'ctx', [(i, i ^ step) for i in range(ranks)])  18.9 us
    ppermute x11, waiting for transfers between devices, exchange(): return lax.ppermute(value, 'ctx', [(i, i ^ step) for i in range(ranks)])  10.7 us
    pallas_call x1, Pallas kernels, per_device(): pl.pallas_call(functools.partial(own_kernel, scale), out_shape=(pltpu.VME...  2.72 us
    pallas_call x1, Pallas kernels, per_device(): pl.pallas_call(functools.partial(gate_kernel, gate_scale, len(packed)), o...  1.8 us
    unnamed x5, local copies, waits for them, and re-layouts  0.94 us
    pallas_call x1, Pallas kernels, per_device(): pl.pallas_call(functools.partial(late_kernel, scale, gate_scale, direct_s...  0.93 us
  transfers between devices with their start and end apart: 11, of which 7 were waited for; matrix products, arithmetic and copies ran while one was open for 0% of the time, Pallas kernels for 8%

profile of v2, /device:TPU:0, one launch (start us, length us, event | category | flops | bytes accessed | tf_op | source)
XLA Modules:
  0.0 37.0 jit_solution(2547647780160267110)
XLA Ops:
  0.6 0.9 %copy.12 = bf16[32,8,2,128]{3,1,2,0:T(8,128)(2,1)S(1)} copy(bf16[32,8,2,128]{3,2,1,0:T(2,128)(2,1)} %bitcast.10) | data formatting | bytes 262144
  1.6 0.0 copy-start.1
  1.6 3.1 %collective-permute-start.4 = (bf16[256,256]{1,0:T(8,128)(2,1)S(1)}, bf16[256,256]{1,0:T(8,128)(2,1)S(1)}, u32[]{:S(2)}, u32[]{:S(2)}) collective-permute-start(bf16[256,256]{1,0:T(8,128)(2,1)S(1)} %bitcast.5), channel_id=1, source_target_pairs={{0,4},{2,6},{4,0},{6,2},{8,12},{10,14},{12,8},{14,10},{1,5},{3,7},... | collective-permute-start | bytes 393224 | tf_op jit(solution)/shard_map/ppermute | solution.py:328
  4.7 2.6 %collective-permute-start = (bf16[256,256]{1,0:T(8,128)(2,1)S(1)}, bf16[256,256]{1,0:T(8,128)(2,1)S(1)}, u32[]{:S(2)}, u32[]{:S(2)}) collective-permute-start(bf16[256,256]{1,0:T(8,128)(2,1)S(1)} %bitcast.6), channel_id=1, source_target_pairs={{0,8},{2,10},{4,12},{6,14},{8,0},{10,2},{12,4},{14,6},{1,9},{3,11}... | collective-permute-start | bytes 393224 | tf_op jit(solution)/shard_map/ppermute | solution.py:328
  7.2 1.5 %collective-permute-start.3 = (bf16[256,256]{1,0:T(8,128)(2,1)S(1)}, bf16[256,256]{1,0:T(8,128)(2,1)S(1)}, u32[]{:S(2)}, u32[]{:S(2)}) collective-permute-start(bf16[256,256]{1,0:T(8,128)(2,1)S(1)} %bitcast.7), channel_id=1, source_target_pairs={{0,2},{2,0},{4,6},{6,4},{8,10},{10,8},{12,14},{14,12},{1,3},{3,1},... | collective-permute-start | bytes 393224 | tf_op jit(solution)/shard_map/ppermute | solution.py:328
  8.8 0.0 copy-done.1
  8.8 2.7 %own_key_blocks.1 = (bf16[10,256,128]{2,1,0:T(8,128)(2,1)S(1)}, bf16[10,128,128]{2,1,0:T(8,128)(2,1)S(1)}, f32[10,4,256]{2,1,0:T(4,128)S(1)}, f32[10,4,256]{2,1,...) custom-call(s32[4]{0:T(128)S(1)} %copy-done.1, ...), custom_call_target="tpu_custom_call" | custom-call | tf_op jit(solution)/shard_map/own_key_blocks/pallas_call | solution.py:334
  11.5 0.0 collective-permute-done.4.refs_1_
  11.5 0.6 %collective-permute-start.5 = (bf16[256,256]{1,0:T(8,128)(2,1)S(1)}, bf16[256,256]{1,0:T(8,128)(2,1)S(1)}, u32[]{:S(2)}, u32[]{:S(2)}) collective-permute-start(bf16[256,256]{1,0:T(8,128)(2,1)S(1)} %collective-permute-done.4.refs_1_), channel_id=1, source_target_pairs={{0,2},{2,0},{4,6},{6,4},{8,10},{10,8},{12,14},{14,12},{1,3},{3,1},... | collective-permute-start | bytes 393224 | tf_op jit(solution)/shard_map/ppermute | solution.py:328
  12.1 1.3 %collective-permute-done.refs_0_ = bf16[256,256]{1,0:T(8,128)(2,1)S(1)} collective-permute-done((bf16[256,256]{1,0:T(8,128)(2,1)S(1)}, bf16[256,256]{1,0:T(8,128)(2,1)S(1)}, u32[]{:S(2)}, u32[]{:S(2)}) %collective-permute-start) | collective-permute-done | bytes 131104 | tf_op jit(solution)/shard_map/ppermute | solution.py:328
  13.4 1.4 %collective-permute-start.6 = (bf16[256,256]{1,0:T(8,128)(2,1)S(1)}, bf16[256,256]{1,0:T(8,128)(2,1)S(1)}, u32[]{:S(2)}, u32[]{:S(2)}) collective-permute-start(bf16[256,256]{1,0:T(8,128)(2,1)S(1)} %pass_on.1.refs_3_), channel_id=1, source_target_pairs={{0,6},{2,4},{4,2},{6,0},{8,14},{10,12},{12,10},{14,8},{1,7},{3,5},... | collective-permute-start | bytes 393224 | tf_op jit(solution)/shard_map/ppermute | solution.py:328
  14.8 1.6 %collective-permute-start.2 = (bf16[256,256]{1,0:T(8,128)(2,1)S(1)}, bf16[256,256]{1,0:T(8,128)(2,1)S(1)}, u32[]{:S(2)}, u32[]{:S(2)}) collective-permute-start(bf16[256,256]{1,0:T(8,128)(2,1)S(1)} %pass_on.1.refs_3_), channel_id=1, source_target_pairs={{0,4},{2,6},{4,0},{6,2},{8,12},{10,14},{12,8},{14,10},{1,5},{3,7},... | collective-permute-start | bytes 393224 | tf_op jit(solution)/shard_map/ppermute | solution.py:328
  16.4 0.5 %collective-permute-start.1 = (bf16[256,256]{1,0:T(8,128)(2,1)S(1)}, bf16[256,256]{1,0:T(8,128)(2,1)S(1)}, u32[]{:S(2)}, u32[]{:S(2)}) collective-permute-start(bf16[256,256]{1,0:T(8,128)(2,1)S(1)} %pass_on.1.refs_3_), channel_id=1, source_target_pairs={{0,2},{2,0},{4,6},{6,4},{8,10},{10,8},{12,14},{14,12},{1,3},{3,1},... | collective-permute-start | bytes 393224 | tf_op jit(solution)/shard_map/ppermute | solution.py:328
  16.9 0.0 collective-permute-done.3.refs_0_
  16.9 3.3 %collective-permute-done.5.refs_2_ = bf16[256,256]{1,0:T(8,128)(2,1)S(1)} collective-permute-done((bf16[256,256]{1,0:T(8,128)(2,1)S(1)}, bf16[256,256]{1,0:T(8,128)(2,1)S(1)}, u32[]{:S(2)}, u32[]{:S(2)}) %collective-permute-start.5) | collective-permute-done | bytes 131104 | tf_op jit(solution)/shard_map/ppermute | solution.py:328
  20.2 0.2 direct_key_blocks.1
  20.4 0.0 collective-permute-done.6.refs_0_
  20.4 0.0 copy-start
  20.4 0.1 middle_key_blocks.1
  20.5 0.3 collective-permute-done.2.refs_1_
  20.7 0.8 %collective-permute-done.1.refs_0_ = bf16[256,256]{1,0:T(8,128)(2,1)S(1)} collective-permute-done((bf16[256,256]{1,0:T(8,128)(2,1)S(1)}, bf16[256,256]{1,0:T(8,128)(2,1)S(1)}, u32[]{:S(2)}, u32[]{:S(2)}) %collective-permute-start.1) | collective-permute-done | bytes 131104 | tf_op jit(solution)/shard_map/ppermute | solution.py:328
  21.6 0.0 copy-done
  21.6 0.9 %late_key_blocks.1 = (f32[10,4,32]{2,1,0:T(4,128)S(1)}, bf16[80,128]{1,0:T(8,128)(2,1)S(1)}, bf16[2,32,384]{2,1,0:T(8,128)(2,1)S(1)}, f32[2,32,128]{2,1,0:T(8,128)S(1)}) custom-call(s32[4]{0:T(128)S(4)} %get-tuple-element.22.marker_ref.lengths_ref, bf16[10,256,128]{2,1,0:T(8,128)(2,1)S(1)} %get-tuple-element.23.q_ref, bf16[2,384,128]{2,1,0:T(8,128)(2,1)S(1)} %copy-done, ...), custom_call_target="tpu_custom_call" | custom-call | tf_op jit(solution)/shard_map/late_key_blocks/pallas_call | solution.py:400
  22.5 3.3 %collective-permute-start.7 = (bf16[80,128]{1,0:T(8,128)(2,1)S(1)}, bf16[80,128]{1,0:T(8,128)(2,1)S(1)}, u32[]{:S(2)}, u32[]{:S(2)}) collective-permute-start(bf16[80,128]{1,0:T(8,128)(2,1)S(1)} %get-tuple-element.35.own_ref), channel_id=1, source_target_pairs={{0,2},{2,0},{4,6},{6,4},{8,10},{10,8},{12,14},{14,12},{1,3},{3,1},... | collective-permute-start | bytes 61448 | tf_op jit(solution)/shard_map/ppermute | solution.py:328
  25.8 1.8 %collective-permute-done.7.side_ref = bf16[80,128]{1,0:T(8,128)(2,1)S(1)} collective-permute-done((bf16[80,128]{1,0:T(8,128)(2,1)S(1)}, bf16[80,128]{1,0:T(8,128)(2,1)S(1)}, u32[]{:S(2)}, u32[]{:S(2)}) %collective-permute-start.7) | collective-permute-done | bytes 20512 | tf_op jit(solution)/shard_map/ppermute | solution.py:328
  27.6 2.7 %collective-permute-start.10 = (bf16[2,80,128]{2,1,0:T(8,128)(2,1)S(1)}, bf16[2,80,128]{2,1,0:T(8,128)(2,1)S(1)}, u32[]{:S(2)}, u32[]{:S(2)}) collective-permute-start(bf16[2,80,128]{2,1,0:T(8,128)(2,1)S(1)} %join_neighbours.1.refs_0_), channel_id=1, source_target_pairs={{0,12},{2,14},{4,8},{6,10},{8,4},{10,6},{12,0},{14,2},{1,13},{3,15... | collective-permute-start | bytes 122888 | tf_op jit(solution)/shard_map/ppermute | solution.py:328
  30.3 0.0 collective-permute-start.9
  30.3 1.7 %collective-permute-start.8 = (bf16[2,80,128]{2,1,0:T(8,128)(2,1)S(1)}, bf16[2,80,128]{2,1,0:T(8,128)(2,1)S(1)}, u32[]{:S(2)}, u32[]{:S(2)}) collective-permute-start(bf16[2,80,128]{2,1,0:T(8,128)(2,1)S(1)} %join_neighbours.1.refs_0_), channel_id=1, source_target_pairs={{0,4},{2,6},{4,0},{6,2},{8,12},{10,14},{12,8},{14,10},{1,5},{3,7},... | collective-permute-start | bytes 122888 | tf_op jit(solution)/shard_map/ppermute | solution.py:328
  31.9 1.4 %collective-permute-done.10.refs_3_ = bf16[2,80,128]{2,1,0:T(8,128)(2,1)S(1)} collective-permute-done((bf16[2,80,128]{2,1,0:T(8,128)(2,1)S(1)}, bf16[2,80,128]{2,1,0:T(8,128)(2,1)S(1)}, u32[]{:S(2)}, u32[]{:S(2)}) %collective-permute-start.10) | collective-permute-done | bytes 40992 | tf_op jit(solution)/shard_map/ppermute | solution.py:328
  33.4 1.8 %collective-permute-done.9.refs_2_ = bf16[2,80,128]{2,1,0:T(8,128)(2,1)S(1)} collective-permute-done((bf16[2,80,128]{2,1,0:T(8,128)(2,1)S(1)}, bf16[2,80,128]{2,1,0:T(8,128)(2,1)S(1)}, u32[]{:S(2)}, u32[]{:S(2)}) %collective-permute-start.9) | collective-permute-done | bytes 40992 | tf_op jit(solution)/shard_map/ppermute | solution.py:328
  35.2 0.0 collective-permute-done.8.refs_1_
  35.2 1.8 %gate_gradients.1 = (f32[10,4,32]{2,1,0:T(4,128)}, f32[4,2,128]{2,1,0:T(2,128)}, f32[10,128,128]{2,1,0:T(8,128)}, f32[2,384,128]{2,1,0:T(8,128)}) custom-call(bf16[2,80,128]{2,1,0:T(8,128)(2,1)S(1)} %join_neighbours.1.refs_0_, bf16[2,80,128]{2,1,0:T(8,128)(2,1)S(1)} %collective-permute-done.8.refs_1_, ...), custom_call_target="tpu_custom_call" | custom-call | tf_op jit(solution)/shard_map/gate_gradients/pallas_call | solution.py:437
  (2 shorter events, 0.0 us)
Async XLA Ops:
  1.6 7.2 %copy-start.1 = (s32[4]{0:T(128)S(1)}, s32[4]{0:T(128)}, u32[]{:S(2)}) copy-start(s32[4]{0:T(128)} %lengths_ref.1) | copy-start | bytes 52
  1.6 9.9 %collective-permute-start.4 = (bf16[256,256]{1,0:T(8,128)(2,1)S(1)}, bf16[256,256]{1,0:T(8,128)(2,1)S(1)}, u32[]{:S(2)}, u32[]{:S(2)}) collective-permute-start(bf16[256,256]{1,0:T(8,128)(2,1)S(1)} %bitcast.5), channel_id=1, source_target_pairs={{0,4},{2,6},{4,0},{6,2},{8,12},{10,14},{12,8},{14,10},{1,5},{3,7},... | collective-permute-start | bytes 393224 | tf_op jit(solution)/shard_map/ppermute | solution.py:328
  4.7 8.7 %collective-permute-start = (bf16[256,256]{1,0:T(8,128)(2,1)S(1)}, bf16[256,256]{1,0:T(8,128)(2,1)S(1)}, u32[]{:S(2)}, u32[]{:S(2)}) collective-permute-start(bf16[256,256]{1,0:T(8,128)(2,1)S(1)} %bitcast.6), channel_id=1, source_target_pairs={{0,8},{2,10},{4,12},{6,14},{8,0},{10,2},{12,4},{14,6},{1,9},{3,11}... | collective-permute-start | bytes 393224 | tf_op jit(solution)/shard_map/ppermute | solution.py:328
  7.2 9.6 %collective-permute-start.3 = (bf16[256,256]{1,0:T(8,128)(2,1)S(1)}, bf16[256,256]{1,0:T(8,128)(2,1)S(1)}, u32[]{:S(2)}, u32[]{:S(2)}) collective-permute-start(bf16[256,256]{1,0:T(8,128)(2,1)S(1)} %bitcast.7), channel_id=1, source_target_pairs={{0,2},{2,0},{4,6},{6,4},{8,10},{10,8},{12,14},{14,12},{1,3},{3,1},... | collective-permute-start | bytes 393224 | tf_op jit(solution)/shard_map/ppermute | solution.py:328
  11.5 8.7 %collective-permute-start.5 = (bf16[256,256]{1,0:T(8,128)(2,1)S(1)}, bf16[256,256]{1,0:T(8,128)(2,1)S(1)}, u32[]{:S(2)}, u32[]{:S(2)}) collective-permute-start(bf16[256,256]{1,0:T(8,128)(2,1)S(1)} %collective-permute-done.4.refs_1_), channel_id=1, source_target_pairs={{0,2},{2,0},{4,6},{6,4},{8,10},{10,8},{12,14},{14,12},{1,3},{3,1},... | collective-permute-start | bytes 393224 | tf_op jit(solution)/shard_map/ppermute | solution.py:328
  13.4 7.0 %collective-permute-start.6 = (bf16[256,256]{1,0:T(8,128)(2,1)S(1)}, bf16[256,256]{1,0:T(8,128)(2,1)S(1)}, u32[]{:S(2)}, u32[]{:S(2)}) collective-permute-start(bf16[256,256]{1,0:T(8,128)(2,1)S(1)} %pass_on.1.refs_3_), channel_id=1, source_target_pairs={{0,6},{2,4},{4,2},{6,0},{8,14},{10,12},{12,10},{14,8},{1,7},{3,5},... | collective-permute-start | bytes 393224 | tf_op jit(solution)/shard_map/ppermute | solution.py:328
  14.8 6.0 %collective-permute-start.2 = (bf16[256,256]{1,0:T(8,128)(2,1)S(1)}, bf16[256,256]{1,0:T(8,128)(2,1)S(1)}, u32[]{:S(2)}, u32[]{:S(2)}) collective-permute-start(bf16[256,256]{1,0:T(8,128)(2,1)S(1)} %pass_on.1.refs_3_), channel_id=1, source_target_pairs={{0,4},{2,6},{4,0},{6,2},{8,12},{10,14},{12,8},{14,10},{1,5},{3,7},... | collective-permute-start | bytes 393224 | tf_op jit(solution)/shard_map/ppermute | solution.py:328
  16.4 5.2 %collective-permute-start.1 = (bf16[256,256]{1,0:T(8,128)(2,1)S(1)}, bf16[256,256]{1,0:T(8,128)(2,1)S(1)}, u32[]{:S(2)}, u32[]{:S(2)}) collective-permute-start(bf16[256,256]{1,0:T(8,128)(2,1)S(1)} %pass_on.1.refs_3_), channel_id=1, source_target_pairs={{0,2},{2,0},{4,6},{6,4},{8,10},{10,8},{12,14},{14,12},{1,3},{3,1},... | collective-permute-start | bytes 393224 | tf_op jit(solution)/shard_map/ppermute | solution.py:328
  20.4 1.2 %copy-start = (bf16[2,384,128]{2,1,0:T(8,128)(2,1)S(1)}, bf16[2,384,128]{2,1,0:T(8,128)(2,1)}, u32[]{:S(2)}) copy-start(bf16[2,384,128]{2,1,0:T(8,128)(2,1)} %wk_ref.1) | copy-start | bytes 589828
  22.5 5.0 %collective-permute-start.7 = (bf16[80,128]{1,0:T(8,128)(2,1)S(1)}, bf16[80,128]{1,0:T(8,128)(2,1)S(1)}, u32[]{:S(2)}, u32[]{:S(2)}) collective-permute-start(bf16[80,128]{1,0:T(8,128)(2,1)S(1)} %get-tuple-element.35.own_ref), channel_id=1, source_target_pairs={{0,2},{2,0},{4,6},{6,4},{8,10},{10,8},{12,14},{14,12},{1,3},{3,1},... | collective-permute-start | bytes 61448 | tf_op jit(solution)/shard_map/ppermute | solution.py:328
  27.6 5.8 %collective-permute-start.10 = (bf16[2,80,128]{2,1,0:T(8,128)(2,1)S(1)}, bf16[2,80,128]{2,1,0:T(8,128)(2,1)S(1)}, u32[]{:S(2)}, u32[]{:S(2)}) collective-permute-start(bf16[2,80,128]{2,1,0:T(8,128)(2,1)S(1)} %join_neighbours.1.refs_0_), channel_id=1, source_target_pairs={{0,12},{2,14},{4,8},{6,10},{8,4},{10,6},{12,0},{14,2},{1,13},{3,15... | collective-permute-start | bytes 122888 | tf_op jit(solution)/shard_map/ppermute | solution.py:328
  30.3 4.9 %collective-permute-start.9 = (bf16[2,80,128]{2,1,0:T(8,128)(2,1)S(1)}, bf16[2,80,128]{2,1,0:T(8,128)(2,1)S(1)}, u32[]{:S(2)}, u32[]{:S(2)}) collective-permute-start(bf16[2,80,128]{2,1,0:T(8,128)(2,1)S(1)} %join_neighbours.1.refs_0_), channel_id=1, source_target_pairs={{0,8},{2,10},{4,12},{6,14},{8,0},{10,2},{12,4},{14,6},{1,9},{3,11}... | collective-permute-start | bytes 122888 | tf_op jit(solution)/shard_map/ppermute | solution.py:328
  30.3 4.9 %collective-permute-start.8 = (bf16[2,80,128]{2,1,0:T(8,128)(2,1)S(1)}, bf16[2,80,128]{2,1,0:T(8,128)(2,1)S(1)}, u32[]{:S(2)}, u32[]{:S(2)}) collective-permute-start(bf16[2,80,128]{2,1,0:T(8,128)(2,1)S(1)} %join_neighbours.1.refs_0_), channel_id=1, source_target_pairs={{0,4},{2,6},{4,0},{6,2},{8,12},{10,14},{12,8},{14,10},{1,5},{3,7},... | collective-permute-start | bytes 122888 | tf_op jit(solution)/shard_map/ppermute | solution.py:328

commit v3 on v2

--- a/solution.py
+++ b/solution.py
@@ -258,8 +258,10 @@
 def gate_kernel(scale, count, *refs):
     packed = jnp.concatenate([ref[...].astype(F32) for ref in refs[:count]], axis=0)
     own_targets_ref, pooled_k_ref, key_proj_ref, wq_ref = refs[count : count + 4]
-    targets_ref, key_grad_ref, wq_grad_ref, wk_grad_ref, own_ref = refs[count + 4 :]
-    targets_ref[...] = own_targets_ref[...]
+    targets_out, key_grad_out, wq_grad_out, wk_grad_out = refs[count + 4 : count + 8]
+    own_ref, key_grad_ref, wq_grad_ref, wk_grad_ref, sent = refs[count + 8 :]
+    copies = [pltpu.make_async_copy(own_targets_ref, targets_out, sent.at[0])]
+    copies[0].start()
     ranks, packed_rows, _ = packed.shape
     kv, block_count, _ = pooled_k_ref.shape
     heads, head_size, _ = wq_ref.shape
@@ -302,6 +304,21 @@
         )
         own_ref[...] = key_grad.reshape(ranks, blocks, head_size)
         key_grad_ref[:, group, :] = own_ref[me]
+        heads_here = pl.ds(group * repeats, repeats)
+        copies += [
+            pltpu.make_async_copy(
+                wq_grad_ref.at[heads_here], wq_grad_out.at[heads_here], sent.at[2 + 2 * group]
+            ),
+            pltpu.make_async_copy(
+                wk_grad_ref.at[group], wk_grad_out.at[group], sent.at[3 + 2 * group]
+            ),
+        ]
+        copies[-2].start()
+        copies[-1].start()
+    copies.append(pltpu.make_async_copy(key_grad_ref, key_grad_out, sent.at[1]))
+    copies[-1].start()
+    for copy in copies:
+        copy.wait()
 
 
 def per_device(queries, keys, doc_lengths, gate_query_weight, gate_key_weight):
@@ -443,8 +460,14 @@
             jax.ShapeDtypeStruct(gate_key_weight.shape, F32),
         ),
         in_specs=[vmem] * (4 + len(packed)),
-        out_specs=(vmem,) * 4,
-        scratch_shapes=[pltpu.VMEM((ranks, blocks, head_size), F32)],
+        out_specs=(anywhere,) * 4,
+        scratch_shapes=[
+            pltpu.VMEM((ranks, blocks, head_size), F32),
+            pltpu.VMEM((blocks, kv, head_size), F32),
+            pltpu.VMEM(gate_query_weight.shape, F32),
+            pltpu.VMEM(gate_key_weight.shape, F32),
+            pltpu.SemaphoreType.DMA((2 + 2 * kv,)),
+        ],
         compiler_params=params,
         name="gate_gradients",
     )(

time: 36.7 us -> 36.6 us (level)
  no operation moved by 1% of the time
where the time goes in v3:
time: 36.6 us; the launch traced here: 36.9 us
  starting transfers between devices  18.9 us (52%)
  waiting for transfers between devices  10.7 us (29%)
  Pallas kernels  5.66 us (15%)
  local copies, waits for them, and re-layouts  0.94 us (3%)
  between operations  0.7 us (2%)
    ppermute x11, starting transfers between devices, exchange(): return lax.ppermute(value, 'ctx', [(i, i ^ step) for i in range(ranks)])  18.9 us
    ppermute x11, waiting for transfers between devices, exchange(): return lax.ppermute(value, 'ctx', [(i, i ^ step) for i in range(ranks)])  10.7 us
    pallas_call x1, Pallas kernels, per_device(): pl.pallas_call(functools.partial(own_kernel, scale), out_shape=(pltpu.VME...  2.72 us
    pallas_call x1, Pallas kernels, per_device(): pl.pallas_call(functools.partial(gate_kernel, gate_scale, len(packed)), o...  1.72 us
    unnamed x5, local copies, waits for them, and re-layouts  0.94 us
    pallas_call x1, Pallas kernels, per_device(): pl.pallas_call(functools.partial(late_kernel, scale, gate_scale, direct_s...  0.93 us
  transfers between devices with their start and end apart: 11, of which 7 were waited for; matrix products, arithmetic and copies ran while one was open for 0% of the time, Pallas kernels for 8%

profile of v3, /device:TPU:0, one launch (start us, length us, event | category | flops | bytes accessed | tf_op | source)
XLA Modules:
  0.0 36.9 jit_solution(3904452859599275414)
XLA Ops:
  0.6 0.9 %copy.12 = bf16[32,8,2,128]{3,1,2,0:T(8,128)(2,1)S(1)} copy(bf16[32,8,2,128]{3,2,1,0:T(2,128)(2,1)} %bitcast.10) | data formatting | bytes 262144
  1.6 0.0 copy-start.1
  1.6 3.1 %collective-permute-start.4 = (bf16[256,256]{1,0:T(8,128)(2,1)S(1)}, bf16[256,256]{1,0:T(8,128)(2,1)S(1)}, u32[]{:S(2)}, u32[]{:S(2)}) collective-permute-start(bf16[256,256]{1,0:T(8,128)(2,1)S(1)} %bitcast.5), channel_id=1, source_target_pairs={{0,4},{2,6},{4,0},{6,2},{8,12},{10,14},{12,8},{14,10},{1,5},{3,7},... | collective-permute-start | bytes 393224 | tf_op jit(solution)/shard_map/ppermute | solution.py:345
  4.7 2.6 %collective-permute-start = (bf16[256,256]{1,0:T(8,128)(2,1)S(1)}, bf16[256,256]{1,0:T(8,128)(2,1)S(1)}, u32[]{:S(2)}, u32[]{:S(2)}) collective-permute-start(bf16[256,256]{1,0:T(8,128)(2,1)S(1)} %bitcast.6), channel_id=1, source_target_pairs={{0,8},{2,10},{4,12},{6,14},{8,0},{10,2},{12,4},{14,6},{1,9},{3,11}... | collective-permute-start | bytes 393224 | tf_op jit(solution)/shard_map/ppermute | solution.py:345
  7.2 1.5 %collective-permute-start.3 = (bf16[256,256]{1,0:T(8,128)(2,1)S(1)}, bf16[256,256]{1,0:T(8,128)(2,1)S(1)}, u32[]{:S(2)}, u32[]{:S(2)}) collective-permute-start(bf16[256,256]{1,0:T(8,128)(2,1)S(1)} %bitcast.7), channel_id=1, source_target_pairs={{0,2},{2,0},{4,6},{6,4},{8,10},{10,8},{12,14},{14,12},{1,3},{3,1},... | collective-permute-start | bytes 393224 | tf_op jit(solution)/shard_map/ppermute | solution.py:345
  8.8 0.0 copy-done.1
  8.8 2.7 %own_key_blocks.1 = (bf16[10,256,128]{2,1,0:T(8,128)(2,1)S(1)}, bf16[10,128,128]{2,1,0:T(8,128)(2,1)S(1)}, f32[10,4,256]{2,1,0:T(4,128)S(1)}, f32[10,4,256]{2,1,...) custom-call(s32[4]{0:T(128)S(1)} %copy-done.1, ...), custom_call_target="tpu_custom_call" | custom-call | tf_op jit(solution)/shard_map/own_key_blocks/pallas_call | solution.py:351
  11.5 0.0 collective-permute-done.4.refs_1_
  11.5 0.6 %collective-permute-start.5 = (bf16[256,256]{1,0:T(8,128)(2,1)S(1)}, bf16[256,256]{1,0:T(8,128)(2,1)S(1)}, u32[]{:S(2)}, u32[]{:S(2)}) collective-permute-start(bf16[256,256]{1,0:T(8,128)(2,1)S(1)} %collective-permute-done.4.refs_1_), channel_id=1, source_target_pairs={{0,2},{2,0},{4,6},{6,4},{8,10},{10,8},{12,14},{14,12},{1,3},{3,1},... | collective-permute-start | bytes 393224 | tf_op jit(solution)/shard_map/ppermute | solution.py:345
  12.1 1.3 %collective-permute-done.refs_0_ = bf16[256,256]{1,0:T(8,128)(2,1)S(1)} collective-permute-done((bf16[256,256]{1,0:T(8,128)(2,1)S(1)}, bf16[256,256]{1,0:T(8,128)(2,1)S(1)}, u32[]{:S(2)}, u32[]{:S(2)}) %collective-permute-start) | collective-permute-done | bytes 131104 | tf_op jit(solution)/shard_map/ppermute | solution.py:345
  13.4 1.4 %collective-permute-start.6 = (bf16[256,256]{1,0:T(8,128)(2,1)S(1)}, bf16[256,256]{1,0:T(8,128)(2,1)S(1)}, u32[]{:S(2)}, u32[]{:S(2)}) collective-permute-start(bf16[256,256]{1,0:T(8,128)(2,1)S(1)} %pass_on.1.refs_3_), channel_id=1, source_target_pairs={{0,6},{2,4},{4,2},{6,0},{8,14},{10,12},{12,10},{14,8},{1,7},{3,5},... | collective-permute-start | bytes 393224 | tf_op jit(solution)/shard_map/ppermute | solution.py:345
  14.8 1.6 %collective-permute-start.2 = (bf16[256,256]{1,0:T(8,128)(2,1)S(1)}, bf16[256,256]{1,0:T(8,128)(2,1)S(1)}, u32[]{:S(2)}, u32[]{:S(2)}) collective-permute-start(bf16[256,256]{1,0:T(8,128)(2,1)S(1)} %pass_on.1.refs_3_), channel_id=1, source_target_pairs={{0,4},{2,6},{4,0},{6,2},{8,12},{10,14},{12,8},{14,10},{1,5},{3,7},... | collective-permute-start | bytes 393224 | tf_op jit(solution)/shard_map/ppermute | solution.py:345
  16.4 0.5 %collective-permute-start.1 = (bf16[256,256]{1,0:T(8,128)(2,1)S(1)}, bf16[256,256]{1,0:T(8,128)(2,1)S(1)}, u32[]{:S(2)}, u32[]{:S(2)}) collective-permute-start(bf16[256,256]{1,0:T(8,128)(2,1)S(1)} %pass_on.1.refs_3_), channel_id=1, source_target_pairs={{0,2},{2,0},{4,6},{6,4},{8,10},{10,8},{12,14},{14,12},{1,3},{3,1},... | collective-permute-start | bytes 393224 | tf_op jit(solution)/shard_map/ppermute | solution.py:345
  16.9 0.0 collective-permute-done.3.refs_0_
  16.9 3.3 %collective-permute-done.5.refs_2_ = bf16[256,256]{1,0:T(8,128)(2,1)S(1)} collective-permute-done((bf16[256,256]{1,0:T(8,128)(2,1)S(1)}, bf16[256,256]{1,0:T(8,128)(2,1)S(1)}, u32[]{:S(2)}, u32[]{:S(2)}) %collective-permute-start.5) | collective-permute-done | bytes 131104 | tf_op jit(solution)/shard_map/ppermute | solution.py:345
  20.2 0.2 direct_key_blocks.1
  20.4 0.0 collective-permute-done.6.refs_0_
  20.4 0.0 copy-start
  20.4 0.1 middle_key_blocks.1
  20.5 0.3 collective-permute-done.2.refs_1_
  20.7 0.8 %collective-permute-done.1.refs_0_ = bf16[256,256]{1,0:T(8,128)(2,1)S(1)} collective-permute-done((bf16[256,256]{1,0:T(8,128)(2,1)S(1)}, bf16[256,256]{1,0:T(8,128)(2,1)S(1)}, u32[]{:S(2)}, u32[]{:S(2)}) %collective-permute-start.1) | collective-permute-done | bytes 131104 | tf_op jit(solution)/shard_map/ppermute | solution.py:345
  21.6 0.0 copy-done
  21.6 0.9 %late_key_blocks.1 = (f32[10,4,32]{2,1,0:T(4,128)S(1)}, bf16[80,128]{1,0:T(8,128)(2,1)S(1)}, bf16[2,32,384]{2,1,0:T(8,128)(2,1)S(1)}, f32[2,32,128]{2,1,0:T(8,128)S(1)}) custom-call(s32[4]{0:T(128)S(4)} %get-tuple-element.22.marker_ref.lengths_ref, bf16[10,256,128]{2,1,0:T(8,128)(2,1)S(1)} %get-tuple-element.23.q_ref, bf16[2,384,128]{2,1,0:T(8,128)(2,1)S(1)} %copy-done, ...), custom_call_target="tpu_custom_call" | custom-call | tf_op jit(solution)/shard_map/late_key_blocks/pallas_call | solution.py:417
  22.5 3.3 %collective-permute-start.7 = (bf16[80,128]{1,0:T(8,128)(2,1)S(1)}, bf16[80,128]{1,0:T(8,128)(2,1)S(1)}, u32[]{:S(2)}, u32[]{:S(2)}) collective-permute-start(bf16[80,128]{1,0:T(8,128)(2,1)S(1)} %get-tuple-element.35.own_ref), channel_id=1, source_target_pairs={{0,2},{2,0},{4,6},{6,4},{8,10},{10,8},{12,14},{14,12},{1,3},{3,1},... | collective-permute-start | bytes 61448 | tf_op jit(solution)/shard_map/ppermute | solution.py:345
  25.8 1.8 %collective-permute-done.7.side_ref = bf16[80,128]{1,0:T(8,128)(2,1)S(1)} collective-permute-done((bf16[80,128]{1,0:T(8,128)(2,1)S(1)}, bf16[80,128]{1,0:T(8,128)(2,1)S(1)}, u32[]{:S(2)}, u32[]{:S(2)}) %collective-permute-start.7) | collective-permute-done | bytes 20512 | tf_op jit(solution)/shard_map/ppermute | solution.py:345
  27.6 2.7 %collective-permute-start.10 = (bf16[2,80,128]{2,1,0:T(8,128)(2,1)S(1)}, bf16[2,80,128]{2,1,0:T(8,128)(2,1)S(1)}, u32[]{:S(2)}, u32[]{:S(2)}) collective-permute-start(bf16[2,80,128]{2,1,0:T(8,128)(2,1)S(1)} %join_neighbours.1.refs_0_), channel_id=1, source_target_pairs={{0,12},{2,14},{4,8},{6,10},{8,4},{10,6},{12,0},{14,2},{1,13},{3,15... | collective-permute-start | bytes 122888 | tf_op jit(solution)/shard_map/ppermute | solution.py:345
  30.3 0.0 collective-permute-start.9
  30.3 1.7 %collective-permute-start.8 = (bf16[2,80,128]{2,1,0:T(8,128)(2,1)S(1)}, bf16[2,80,128]{2,1,0:T(8,128)(2,1)S(1)}, u32[]{:S(2)}, u32[]{:S(2)}) collective-permute-start(bf16[2,80,128]{2,1,0:T(8,128)(2,1)S(1)} %join_neighbours.1.refs_0_), channel_id=1, source_target_pairs={{0,4},{2,6},{4,0},{6,2},{8,12},{10,14},{12,8},{14,10},{1,5},{3,7},... | collective-permute-start | bytes 122888 | tf_op jit(solution)/shard_map/ppermute | solution.py:345
  31.9 1.4 %collective-permute-done.10.refs_3_ = bf16[2,80,128]{2,1,0:T(8,128)(2,1)S(1)} collective-permute-done((bf16[2,80,128]{2,1,0:T(8,128)(2,1)S(1)}, bf16[2,80,128]{2,1,0:T(8,128)(2,1)S(1)}, u32[]{:S(2)}, u32[]{:S(2)}) %collective-permute-start.10) | collective-permute-done | bytes 40992 | tf_op jit(solution)/shard_map/ppermute | solution.py:345
  33.4 1.8 %collective-permute-done.9.refs_2_ = bf16[2,80,128]{2,1,0:T(8,128)(2,1)S(1)} collective-permute-done((bf16[2,80,128]{2,1,0:T(8,128)(2,1)S(1)}, bf16[2,80,128]{2,1,0:T(8,128)(2,1)S(1)}, u32[]{:S(2)}, u32[]{:S(2)}) %collective-permute-start.9) | collective-permute-done | bytes 40992 | tf_op jit(solution)/shard_map/ppermute | solution.py:345
  35.2 0.0 collective-permute-done.8.refs_1_
  35.2 1.7 %gate_gradients.1 = (f32[10,4,32]{2,1,0:T(4,128)}, f32[4,2,128]{2,1,0:T(2,128)}, f32[10,128,128]{2,1,0:T(8,128)}, f32[2,384,128]{2,1,0:T(8,128)}) custom-call(bf16[2,80,128]{2,1,0:T(8,128)(2,1)S(1)} %join_neighbours.1.refs_0_, bf16[2,80,128]{2,1,0:T(8,128)(2,1)S(1)} %collective-permute-done.8.refs_1_, ...), custom_call_target="tpu_custom_call" | custom-call | tf_op jit(solution)/shard_map/gate_gradients/pallas_call | solution.py:454
  (2 shorter events, 0.0 us)
Async XLA Ops:
  1.6 7.2 %copy-start.1 = (s32[4]{0:T(128)S(1)}, s32[4]{0:T(128)}, u32[]{:S(2)}) copy-start(s32[4]{0:T(128)} %lengths_ref.1) | copy-start | bytes 52
  1.6 9.9 %collective-permute-start.4 = (bf16[256,256]{1,0:T(8,128)(2,1)S(1)}, bf16[256,256]{1,0:T(8,128)(2,1)S(1)}, u32[]{:S(2)}, u32[]{:S(2)}) collective-permute-start(bf16[256,256]{1,0:T(8,128)(2,1)S(1)} %bitcast.5), channel_id=1, source_target_pairs={{0,4},{2,6},{4,0},{6,2},{8,12},{10,14},{12,8},{14,10},{1,5},{3,7},... | collective-permute-start | bytes 393224 | tf_op jit(solution)/shard_map/ppermute | solution.py:345
  4.7 8.7 %collective-permute-start = (bf16[256,256]{1,0:T(8,128)(2,1)S(1)}, bf16[256,256]{1,0:T(8,128)(2,1)S(1)}, u32[]{:S(2)}, u32[]{:S(2)}) collective-permute-start(bf16[256,256]{1,0:T(8,128)(2,1)S(1)} %bitcast.6), channel_id=1, source_target_pairs={{0,8},{2,10},{4,12},{6,14},{8,0},{10,2},{12,4},{14,6},{1,9},{3,11}... | collective-permute-start | bytes 393224 | tf_op jit(solution)/shard_map/ppermute | solution.py:345
  7.2 9.6 %collective-permute-start.3 = (bf16[256,256]{1,0:T(8,128)(2,1)S(1)}, bf16[256,256]{1,0:T(8,128)(2,1)S(1)}, u32[]{:S(2)}, u32[]{:S(2)}) collective-permute-start(bf16[256,256]{1,0:T(8,128)(2,1)S(1)} %bitcast.7), channel_id=1, source_target_pairs={{0,2},{2,0},{4,6},{6,4},{8,10},{10,8},{12,14},{14,12},{1,3},{3,1},... | collective-permute-start | bytes 393224 | tf_op jit(solution)/shard_map/ppermute | solution.py:345
  11.5 8.7 %collective-permute-start.5 = (bf16[256,256]{1,0:T(8,128)(2,1)S(1)}, bf16[256,256]{1,0:T(8,128)(2,1)S(1)}, u32[]{:S(2)}, u32[]{:S(2)}) collective-permute-start(bf16[256,256]{1,0:T(8,128)(2,1)S(1)} %collective-permute-done.4.refs_1_), channel_id=1, source_target_pairs={{0,2},{2,0},{4,6},{6,4},{8,10},{10,8},{12,14},{14,12},{1,3},{3,1},... | collective-permute-start | bytes 393224 | tf_op jit(solution)/shard_map/ppermute | solution.py:345
  13.4 7.0 %collective-permute-start.6 = (bf16[256,256]{1,0:T(8,128)(2,1)S(1)}, bf16[256,256]{1,0:T(8,128)(2,1)S(1)}, u32[]{:S(2)}, u32[]{:S(2)}) collective-permute-start(bf16[256,256]{1,0:T(8,128)(2,1)S(1)} %pass_on.1.refs_3_), channel_id=1, source_target_pairs={{0,6},{2,4},{4,2},{6,0},{8,14},{10,12},{12,10},{14,8},{1,7},{3,5},... | collective-permute-start | bytes 393224 | tf_op jit(solution)/shard_map/ppermute | solution.py:345
  14.8 6.0 %collective-permute-start.2 = (bf16[256,256]{1,0:T(8,128)(2,1)S(1)}, bf16[256,256]{1,0:T(8,128)(2,1)S(1)}, u32[]{:S(2)}, u32[]{:S(2)}) collective-permute-start(bf16[256,256]{1,0:T(8,128)(2,1)S(1)} %pass_on.1.refs_3_), channel_id=1, source_target_pairs={{0,4},{2,6},{4,0},{6,2},{8,12},{10,14},{12,8},{14,10},{1,5},{3,7},... | collective-permute-start | bytes 393224 | tf_op jit(solution)/shard_map/ppermute | solution.py:345
  16.4 5.2 %collective-permute-start.1 = (bf16[256,256]{1,0:T(8,128)(2,1)S(1)}, bf16[256,256]{1,0:T(8,128)(2,1)S(1)}, u32[]{:S(2)}, u32[]{:S(2)}) collective-permute-start(bf16[256,256]{1,0:T(8,128)(2,1)S(1)} %pass_on.1.refs_3_), channel_id=1, source_target_pairs={{0,2},{2,0},{4,6},{6,4},{8,10},{10,8},{12,14},{14,12},{1,3},{3,1},... | collective-permute-start | bytes 393224 | tf_op jit(solution)/shard_map/ppermute | solution.py:345
  20.4 1.2 %copy-start = (bf16[2,384,128]{2,1,0:T(8,128)(2,1)S(1)}, bf16[2,384,128]{2,1,0:T(8,128)(2,1)}, u32[]{:S(2)}) copy-start(bf16[2,384,128]{2,1,0:T(8,128)(2,1)} %wk_ref.1) | copy-start | bytes 589828
  22.5 5.0 %collective-permute-start.7 = (bf16[80,128]{1,0:T(8,128)(2,1)S(1)}, bf16[80,128]{1,0:T(8,128)(2,1)S(1)}, u32[]{:S(2)}, u32[]{:S(2)}) collective-permute-start(bf16[80,128]{1,0:T(8,128)(2,1)S(1)} %get-tuple-element.35.own_ref), channel_id=1, source_target_pairs={{0,2},{2,0},{4,6},{6,4},{8,10},{10,8},{12,14},{14,12},{1,3},{3,1},... | collective-permute-start | bytes 61448 | tf_op jit(solution)/shard_map/ppermute | solution.py:345
  27.6 5.8 %collective-permute-start.10 = (bf16[2,80,128]{2,1,0:T(8,128)(2,1)S(1)}, bf16[2,80,128]{2,1,0:T(8,128)(2,1)S(1)}, u32[]{:S(2)}, u32[]{:S(2)}) collective-permute-start(bf16[2,80,128]{2,1,0:T(8,128)(2,1)S(1)} %join_neighbours.1.refs_0_), channel_id=1, source_target_pairs={{0,12},{2,14},{4,8},{6,10},{8,4},{10,6},{12,0},{14,2},{1,13},{3,15... | collective-permute-start | bytes 122888 | tf_op jit(solution)/shard_map/ppermute | solution.py:345
  30.3 4.9 %collective-permute-start.9 = (bf16[2,80,128]{2,1,0:T(8,128)(2,1)S(1)}, bf16[2,80,128]{2,1,0:T(8,128)(2,1)S(1)}, u32[]{:S(2)}, u32[]{:S(2)}) collective-permute-start(bf16[2,80,128]{2,1,0:T(8,128)(2,1)S(1)} %join_neighbours.1.refs_0_), channel_id=1, source_target_pairs={{0,8},{2,10},{4,12},{6,14},{8,0},{10,2},{12,4},{14,6},{1,9},{3,11}... | collective-permute-start | bytes 122888 | tf_op jit(solution)/shard_map/ppermute | solution.py:345
  30.3 4.9 %collective-permute-start.8 = (bf16[2,80,128]{2,1,0:T(8,128)(2,1)S(1)}, bf16[2,80,128]{2,1,0:T(8,128)(2,1)S(1)}, u32[]{:S(2)}, u32[]{:S(2)}) collective-permute-start(bf16[2,80,128]{2,1,0:T(8,128)(2,1)S(1)} %join_neighbours.1.refs_0_), channel_id=1, source_target_pairs={{0,4},{2,6},{4,0},{6,2},{8,12},{10,14},{12,8},{14,10},{1,5},{3,7},... | collective-permute-start | bytes 122888 | tf_op jit(solution)/shard_map/ppermute | solution.py:345
